TPU v7x, 32 devices: a whole 2x2x4 slice. The times are simulated.
32 devices in a mesh: img: 8 (over z, x), head: 4 (over y, core).
Axes of the slice: x: 2, y: 2, z: 4, core: 2. Of those that a mesh axis runs over, the one named last changes fastest.
Arguments:
- media_tokens: bfloat16 [256, 576, 1024], P(('img', 'head')), may hold values from -6 to 6
- latents: bfloat16 [256, 64, 1024], P(('img', 'head')), may hold values from -6 to 6
- lengths: int32 [256], P('img'), may hold values from 144 to 576, as said below
- query_weight: bfloat16 [1024, 512], replicated, may hold values from -0.1875 to 0.1875
- keyval_weight: bfloat16 [1024, 1024], replicated, may hold values from -0.1875 to 0.1875
- output_weight: bfloat16 [512, 1024], replicated, may hold values from -3 to 3
- inner_weight: bfloat16 [1024, 4096], replicated, may hold values from -0.1875 to 0.1875
- outer_weight: bfloat16 [4096, 1024], replicated, may hold values from -0.09375 to 0.09375
- media_gain: float32 [1024], replicated, may hold values from 0.25 to 1.75
- media_bias: float32 [1024], replicated, may hold values from -0.4375 to 0.4375
- latent_gain: float32 [1024], replicated, may hold values from 0.25 to 1.75
- latent_bias: float32 [1024], replicated, may hold values from -0.4375 to 0.4375
- feed_gain: float32 [1024], replicated, may hold values from 0.25 to 1.75
- feed_bias: float32 [1024], replicated, may hold values from -4 to 4
- cotangent: bfloat16 [256, 64, 1024], P(('img', 'head')), may hold values from -6 to 6
Outputs:
- out_latents: bfloat16 [256, 64, 1024], P(('img', 'head'))
- grad_media: bfloat16 [256, 576, 1024], P(('img', 'head'))
- grad_latents: bfloat16 [256, 64, 1024], P(('img', 'head'))
- grad_query: float32 [1024, 512], P(('img', 'head'))
- grad_keyval: float32 [1024, 1024], P(('img', 'head'))
- grad_output: float32 [512, 1024], P(('img', 'head'))
- grad_inner: float32 [1024, 4096], P(('img', 'head'))
- grad_outer: float32 [4096, 1024], P(('img', 'head'))
- grad_media_gain: float32 [1024], P(('img', 'head'))
- grad_media_bias: float32 [1024], P(('img', 'head'))
- grad_latent_gain: float32 [1024], P(('img', 'head'))
- grad_latent_bias: float32 [1024], P(('img', 'head'))
- grad_feed_gain: float32 [1024], P(('img', 'head'))
- grad_feed_bias: float32 [1024], P(('img', 'head'))
Inputs may be any that keep to these rules, and one draw needn't show every extreme that they name: `lengths`: valid media positions of each image; some image has exactly 576.
All inputs are finite; a program needn't handle non-finite values.
Results may differ from a plain program's by a relative error of at most 0.014.
Values may be sent and summed in bfloat16 or wider, within the bound.
No kernel may reach another device: no remote copies, remote signals or barrier semaphores. Data moves between devices by JAX's collectives and lax.ppermute only.
A program may use at most 320 MiB of HBM per device.

v0:
```python
from functools import partial

import jax
import jax.numpy as jnp
from jax import lax
from jax.sharding import PartitionSpec as P

HEAD_DIM = 64


norm_eps = 1e-05
masked_score = -1e30


def layer_norm(values, norm_gain, norm_bias):
    centre = values - jnp.mean(values, axis=-1, keepdims=True)
    spread = jnp.mean(centre * centre, axis=-1, keepdims=True)
    return centre * lax.rsqrt(spread + norm_eps) * norm_gain + norm_bias


def project(left_rows, weight):
    return jnp.einsum("ind,de->ine", left_rows, weight, preferred_element_type=jnp.float32)


def project_back(left_rows, weight):
    return jnp.einsum("ine,de->ind", left_rows, weight, preferred_element_type=jnp.float32)


def outer_product(left_rows, right_rows):
    return jnp.einsum("ind,ine->de", left_rows, right_rows, preferred_element_type=jnp.float32)


def head_view(matrix):
    return matrix.reshape(matrix.shape[0], matrix.shape[1], matrix.shape[2] // HEAD_DIM, HEAD_DIM)


def masked_scores(query_heads, key_heads, length_rows):
    scores = jnp.einsum(
        "iahc,ijhc->ihaj",
        head_view(query_heads),
        head_view(key_heads),
        preferred_element_type=jnp.float32,
    )
    key_count = key_heads.shape[1]
    media_rows = key_count - query_heads.shape[1]
    position = lax.broadcasted_iota(jnp.int32, (1, 1, 1, key_count), 3)
    usable = (position < length_rows[:, None, None, None]) | (position >= media_rows)
    return jnp.where(usable, scores, masked_score)


def attend(query_heads, key_heads, value_heads, length_rows):
    scores = masked_scores(query_heads, key_heads, length_rows)
    row_top = jnp.max(scores, axis=-1, keepdims=True)
    log_total = row_top + jnp.log(jnp.sum(jnp.exp(scores - row_top), axis=-1, keepdims=True))
    prob_rows = jnp.exp(scores - log_total)
    prob_low = prob_rows.astype(jnp.bfloat16)
    mixed_heads = jnp.einsum(
        "ihaj,ijhc->iahc", prob_low, head_view(value_heads), preferred_element_type=jnp.float32
    )
    mixed_heads = mixed_heads.reshape(query_heads.shape).astype(jnp.bfloat16)
    return (prob_rows, prob_low, mixed_heads)


def attend_back(query_heads, key_heads, value_heads, prob_rows, prob_low, grad_heads):
    grad_view = head_view(grad_heads)
    prob_grad = jnp.einsum(
        "iahc,ijhc->ihaj", grad_view, head_view(value_heads), preferred_element_type=jnp.float32
    )
    value_grad = jnp.einsum(
        "ihaj,iahc->ijhc", prob_low, grad_view, preferred_element_type=jnp.float32
    )
    value_grad = value_grad.reshape(value_heads.shape).astype(jnp.bfloat16)
    score_grad = prob_rows * (prob_grad - jnp.sum(prob_rows * prob_grad, axis=-1, keepdims=True))
    score_grad = score_grad.astype(jnp.bfloat16)
    query_grad = jnp.einsum(
        "ihaj,ijhc->iahc", score_grad, head_view(key_heads), preferred_element_type=jnp.float32
    )
    query_grad = query_grad.reshape(query_heads.shape).astype(jnp.bfloat16)
    key_grad = jnp.einsum(
        "ihaj,iahc->ijhc", score_grad, head_view(query_heads), preferred_element_type=jnp.float32
    )
    key_grad = key_grad.reshape(key_heads.shape).astype(jnp.bfloat16)
    return (query_grad, key_grad, value_grad)


def on_device(
    media_tokens,
    latents,
    lengths,
    query_weight,
    keyval_weight,
    output_weight,
    inner_weight,
    outer_weight,
    media_gain,
    media_bias,
    latent_gain,
    latent_bias,
    feed_gain,
    feed_bias,
    cotangent,
):
    media_in = media_tokens.astype(jnp.float32)
    latent_in = latents.astype(jnp.float32)
    media_norm, media_pull = jax.vjp(layer_norm, media_in, media_gain, media_bias)
    latent_norm, latent_pull = jax.vjp(layer_norm, latent_in, latent_gain, latent_bias)
    media_low = media_norm.astype(jnp.bfloat16)
    latent_low = latent_norm.astype(jnp.bfloat16)
    query_rows = (project(latent_low, query_weight) * 0.125).astype(jnp.bfloat16)
    keyval_in = jnp.concatenate([media_low, latent_low], axis=1)
    keyval = project(keyval_in, keyval_weight)
    inner_width = query_weight.shape[1]
    key_rows = keyval[..., :inner_width].astype(jnp.bfloat16)
    value_rows = keyval[..., inner_width:].astype(jnp.bfloat16)
    query_heads, key_heads, value_heads = (
        lax.all_to_all(query_rows, "head", split_axis=2, concat_axis=0, tiled=True),
        lax.all_to_all(key_rows, "head", split_axis=2, concat_axis=0, tiled=True),
        lax.all_to_all(value_rows, "head", split_axis=2, concat_axis=0, tiled=True),
    )
    prob_rows, prob_low, mixed_heads = attend(query_heads, key_heads, value_heads, lengths)
    mixed_rows = lax.all_to_all(mixed_heads, "head", split_axis=0, concat_axis=2, tiled=True)
    residual = latent_in + project(mixed_rows, output_weight)
    hidden_norm, feed_pull = jax.vjp(layer_norm, residual, feed_gain, feed_bias)
    hidden_low = hidden_norm.astype(jnp.bfloat16)
    inner_rows = project(hidden_low, inner_weight)
    activation, gelu_pull = jax.vjp(partial(jax.nn.gelu, approximate=False), inner_rows)
    activation_low = activation.astype(jnp.bfloat16)
    out_latents = (residual + project(activation_low, outer_weight)).astype(jnp.bfloat16)
    grad_outer = outer_product(activation_low, cotangent)
    activation_grad = project_back(cotangent, outer_weight)
    inner_grad = gelu_pull(activation_grad)[0].astype(jnp.bfloat16)
    grad_inner = outer_product(hidden_low, inner_grad)
    hidden_grad = project_back(inner_grad, inner_weight)
    residual_part, feed_gain_grad, feed_bias_grad = feed_pull(hidden_grad)
    residual_grad = cotangent.astype(jnp.float32) + residual_part
    residual_low = residual_grad.astype(jnp.bfloat16)
    grad_output = outer_product(mixed_rows, residual_low)
    mixed_grad = project_back(residual_low, output_weight).astype(jnp.bfloat16)
    mixed_grad_heads = lax.all_to_all(mixed_grad, "head", split_axis=2, concat_axis=0, tiled=True)
    query_grad, key_grad, value_grad = attend_back(
        query_heads, key_heads, value_heads, prob_rows, prob_low, mixed_grad_heads
    )
    query_back, key_back, value_back = (
        lax.all_to_all(query_grad, "head", split_axis=0, concat_axis=2, tiled=True),
        lax.all_to_all(key_grad, "head", split_axis=0, concat_axis=2, tiled=True),
        lax.all_to_all(value_grad, "head", split_axis=0, concat_axis=2, tiled=True),
    )
    grad_query = outer_product(latent_low, query_back) * 0.125
    keyval_back = jnp.concatenate([key_back, value_back], axis=2)
    grad_keyval = outer_product(keyval_in, keyval_back)
    keyval_in_grad = project_back(keyval_back, keyval_weight)
    media_rows = media_tokens.shape[1]
    latent_norm_grad = (
        keyval_in_grad[:, media_rows:] + project_back(query_back, query_weight) * 0.125
    )
    media_grad, media_gain_grad, media_bias_grad = media_pull(keyval_in_grad[:, :media_rows])
    latent_part, latent_gain_grad, latent_bias_grad = latent_pull(latent_norm_grad)
    grad_media = media_grad.astype(jnp.bfloat16)
    grad_latents = (residual_grad + latent_part).astype(jnp.bfloat16)
    shares = (
        lax.psum_scatter(grad_query, ("img", "head"), scatter_dimension=0, tiled=True),
        lax.psum_scatter(grad_keyval, ("img", "head"), scatter_dimension=0, tiled=True),
        lax.psum_scatter(grad_output, ("img", "head"), scatter_dimension=0, tiled=True),
        lax.psum_scatter(grad_inner, ("img", "head"), scatter_dimension=0, tiled=True),
        lax.psum_scatter(grad_outer, ("img", "head"), scatter_dimension=0, tiled=True),
        lax.psum_scatter(media_gain_grad, ("img", "head"), scatter_dimension=0, tiled=True),
        lax.psum_scatter(media_bias_grad, ("img", "head"), scatter_dimension=0, tiled=True),
        lax.psum_scatter(latent_gain_grad, ("img", "head"), scatter_dimension=0, tiled=True),
        lax.psum_scatter(latent_bias_grad, ("img", "head"), scatter_dimension=0, tiled=True),
        lax.psum_scatter(feed_gain_grad, ("img", "head"), scatter_dimension=0, tiled=True),
        lax.psum_scatter(feed_bias_grad, ("img", "head"), scatter_dimension=0, tiled=True),
    )
    return (
        out_latents,
        grad_media,
        grad_latents,
        shares[0],
        shares[1],
        shares[2],
        shares[3],
        shares[4],
        shares[5],
        shares[6],
        shares[7],
        shares[8],
        shares[9],
        shares[10],
    )


def solution(mesh):
    return jax.shard_map(
        on_device,
        mesh=mesh,
        in_specs=(
            P(("img", "head"), None, None),
            P(("img", "head"), None, None),
            P("img"),
            P(),
            P(),
            P(),
            P(),
            P(),
            P(),
            P(),
            P(),
            P(),
            P(),
            P(),
            P(("img", "head"), None, None),
        ),
        out_specs=(
            P(("img", "head"), None, None),
            P(("img", "head"), None, None),
            P(("img", "head"), None, None),
            P(("img", "head"), None),
            P(("img", "head"), None),
            P(("img", "head"), None),
            P(("img", "head"), None),
            P(("img", "head"), None),
            P(("img", "head")),
            P(("img", "head")),
            P(("img", "head")),
            P(("img", "head")),
            P(("img", "head")),
            P(("img", "head")),
        ),
        check_vma=False,
    )
```

profile of v0, /device:TPU:0, one launch (start us, length us, event | category | flops | bytes accessed | tf_op | source)
XLA Modules:
  0.0 1157.7 jit_solution(15860496543871347330)
XLA Ops:
  39.4 17.5 %fusion.29 = bf16[8,640,1024]{2,1,0:T(8,128)(2,1)} fusion(bf16[8,64,1024]{2,1,0:T(8,128)(2,1)S(1)} %copy-done.19, bf16[8,576,1024]{2,1,0:T(8,128)(2,1)} %fusion.7, bf16[1024,1024]{1,0:T(8,128)(2,1)S(1)} %copy-done), kind=kOutput, calls=%fused_computation.57 | convolution fusion | flops 10763632640 | bytes 23068672 | tf_op jit(solution)/shard_map/ind,de->ine/dot_general | solution.py:22
  56.9 8.9 fusion.71
  65.8 9.2 copy.55
  80.3 9.2 copy.51
  89.5 50.2 %all-to-all-done.2 = bf16[8,640,512]{1,0,2:T(8,128)(2,1)} async-done(((bf16[8,640,512]{1,0,2:T(8,128)(2,1)}), bf16[8,640,512]{1,0,2:T(8,128)(2,1)}, u32[]{:S(2)}, u32[]{:S(2)}) %all-to-all-start.2) | async-done | bytes 5242912 | tf_op jit(solution)/shard_map/all_to_all | solution.py:117
  154.3 50.0 %all-to-all-done = bf16[8,640,512]{1,0,2:T(8,128)(2,1)} async-done(((bf16[8,640,512]{1,0,2:T(8,128)(2,1)}), bf16[8,640,512]{1,0,2:T(8,128)(2,1)}, u32[]{:S(2)}, u32[]{:S(2)}) %all-to-all-start) | async-done | bytes 5242912 | tf_op jit(solution)/shard_map/all_to_all | solution.py:118
  224.6 12.7 %all_to_all.132 = bf16[32,64,128]{2,1,0:T(8,128)(2,1)S(1)} all-to-all(bf16[32,64,128]{2,1,0:T(8,128)(2,1)} %copy.58), channel_id=1, replica_groups=mesh['img'=8,'head'=4] {'head'}, dimensions={0} | all-to-all | bytes 1048576 | tf_op jit(solution)/shard_map/all_to_all | solution.py:121
  243.1 9.4 fusion.48
  252.5 19.8 %multiply_convert_fusion.1 = (bf16[8,64,4096]{2,1,0:T(8,128)(2,1)}, f32[8,64,4096]{2,1,0:T(8,128)}) fusion(f32[8,64,4096]{2,1,0:T(8,128)S(1)} %get-tuple-element.42, u8[64,4096]{1,0:T(8,128)(4,1)S(1)} %get-tuple-element.18, u8[64,4096]{1,0:T(8,128)(4,1)S(1)} %get-tuple-element.17), kind=kLoop, calls=%fused_computation.40 | loop fusion | flops 146800640 | bytes 21495808 | tf_op jit(solution)/shard_map/convert_element_type | solution.py:127
  272.3 12.0 %add_convert_fusion.1 = bf16[8,64,4096]{2,1,0:T(8,128)(2,1)} fusion(f32[8,64,4096]{2,1,0:T(8,128)} %get-tuple-element.35, f32[8,64,4096]{2,1,0:T(8,128)S(1)} %get-tuple-element.42, bf16[8,64,1024]{2,1,0:T(8,128)(2,1)} %param.29, bf16[4096,1024]{1,0:T(8,128)(2,1)} %param.22), kind=kOutput, calls=%fused_computation.39 | convolution fusion | flops 4324327424 | bytes 30408704 | tf_op jit(solution)/shard_map/ine,de->ind/dot_general | solution.py:26
  284.3 9.5 multiply_reduce_fusion.1
  302.2 13.0 %all_to_all.133 = bf16[4,2,32768]{2,1,0:T(2,128)(2,1)} all-to-all(bf16[4,2,32768]{2,1,0:T(2,128)(2,1)} %reshape.219), channel_id=1, replica_groups=mesh['img'=8,'head'=4] {'head'}, dimensions={0} | all-to-all | bytes 1048576 | tf_op jit(solution)/shard_map/all_to_all | solution.py:139
  319.5 11.4 multiply_reduce_fusion
  345.9 9.2 convolution_convert_fusion
  371.0 59.3 %all-to-all-done.6 = bf16[32,640,128]{1,2,0:T(8,128)(2,1)} async-done(((bf16[32,640,128]{1,2,0:T(8,128)(2,1)}), bf16[32,640,128]{1,2,0:T(8,128)(2,1)}, u32[]{:S(2)}, u32[]{:S(2)}) %all-to-all-start.6) | async-done | bytes 5242912 | tf_op jit(solution)/shard_map/all_to_all | solution.py:146
  439.8 9.6 copy.66
  449.4 8.7 all_to_all.119
  458.1 47.1 %all-to-all-done.5 = bf16[32,640,128]{1,2,0:T(8,128)(2,1)} async-done(((bf16[32,640,128]{1,2,0:T(8,128)(2,1)}), bf16[32,640,128]{1,2,0:T(8,128)(2,1)}, u32[]{:S(2)}, u32[]{:S(2)}) %all-to-all-start.5) | async-done | bytes 5242912 | tf_op jit(solution)/shard_map/all_to_all | solution.py:145
  505.2 9.3 copy.64
  514.5 8.8 all_to_all.115
  531.6 17.9 %fusion.38 = f32[1024,1024]{1,0:T(8,128)} fusion(bf16[8,640,1024]{2,1,0:T(8,128)(2,1)} %constant_dynamic-update-slice_fusion, bf16[8,64,1024]{2,1,0:T(8,128)(2,1)S(1)} %copy-done.20, bf16[8,576,1024]{2,1,0:T(8,128)(2,1)} %fusion.7), kind=kOutput, calls=%fused_computation.71 | convolution fusion | flops 10758389760 | bytes 25165824 | tf_op jit(solution)/shard_map/ind,ine->de/dot_general | solution.py:30
  549.6 13.4 %convolution_bitcast_fusion.1 = f32[1024,4096]{1,0:T(8,128)} fusion(bf16[8,64,4096]{2,1,0:T(8,128)(2,1)} %add_convert_fusion.1, f32[8,64,1024]{2,1,0:T(8,128)} %copy-done.7, f32[1024]{0:T(1024)S(1)} %copy-done.49, f32[1024]{0:T(1024)S(1)} %copy-done.45, f32[8,64]{1,0:T(8,128)S(1)} %fusion.63, f32[8,64]{1,0:T(8,128)S(1)} %broadcast_multiply_fusion.1), kind=kOutput, calls=%fused_computation.24 | convolution fusion | flops 4297588736 | bytes 23080960 | tf_op jit(solution)/shard_map/ind,ine->de/dot_general | solution.py:30
  564.3 10.5 convolution_bitcast_fusion
  574.9 10.8 add_convert_fusion.3
  585.8 17.9 %fusion.44 = f32[8,640,1024]{2,1,0:T(8,128)} fusion(bf16[8,640,1024]{2,1,0:T(8,128)(2,1)} %constant_dynamic-update-slice_fusion, bf16[1024,1024]{1,0:T(8,128)(2,1)S(1)} %copy-done), kind=kOutput, calls=%fused_computation.79 | convolution fusion | flops 10737418240 | bytes 33554432 | tf_op jit(solution)/shard_map/ine,de->ind/dot_general | solution.py:26
  606.5 9.1 fusion.10
  616.7 13.0 %fusion.8 = (f32[1024]{0:T(1024)S(1)}, f32[8,576]{1,0:T(8,128)S(1)}, f32[1024]{0:T(1024)S(1)}) fusion(bf16[8,576,1024]{2,1,0:T(8,128)(2,1)S(1)} %bitcast.123, f32[8,640,1024]{2,1,0:T(8,128)} %fusion.44, f32[8,576]{1,0:T(8,128)S(1)} %copy-done.29, f32[8,576]{1,0:T(8,128)S(1)} %copy-done.25, f32[8,576]{1,0:T(8,128)S(1)} %multiply_multiply_fusion.5, ...), kind=kLoop, calls=%fused_computation.11 | loop fusion | flops 56616448 | bytes 28397568 | tf_op jit(solution)/shard_map/transpose(jvp())/reduce_sum | solution.py:18
  629.8 40.9 %all-reduce.6 = (f32[1024]{0:T(1024)S(1)}, f32[1024]{0:T(1024)S(1)}, f32[1024]{0:T(1024)S(1)}, f32[1024]{0:T(1024)S(1)}, f32[1024]{0:T(1024)S(1)}, /*index=5*/f32[1024]{0:T(1024)S(1)}) all-reduce(f32[1024]{0:T(1024)S(1)} %get-tuple-element.14, ...), channel_id=7, replica_groups=mesh['img'=8,'head'=4] {'img','head'}, use_global_device_ids=true, to_apply=%region_21.22.clone | all-reduce | flops 6144 | bytes 49152
  678.0 15.3 %add_convert_fusion = bf16[8,576,1024]{2,1,0:T(8,128)(2,1)} fusion(f32[8,576]{1,0:T(8,128)S(1)} %negate_multiply_fusion.1, f32[8,576]{1,0:T(8,128)S(1)} %multiply_multiply_fusion.5, f32[8,576]{1,0:T(8,128)S(1)} %copy-done.25, bf16[8,576,1024]{2,1,0:T(8,128)(2,1)} %param.15, f32[8,576]{1,0:T(8,128)S(1)} %copy-done.29, f32[1024]{0:T(1024)S(1)} %copy-done.37, ...), kind=kLoop, calls=%fused_computation.14 | loop fusion | flops 42467328 | bytes 37826560 | tf_op jit(solution)/shard_map/convert_element_type | solution.py:158
  693.3 88.7 %reduce-scatter.8.cloned.1.call-done = f32[32,1024]{1,0:T(8,128)} async-done(((f32[1024,1024]{1,0:T(8,128)}), f32[32,1024]{1,0:T(8,128)}) %reduce-scatter.8.cloned.1.call-update) | async-done | bytes 131088 | tf_op jit(solution)/shard_map/reduce_scatter | solution.py:162
  782.0 181.6 %reduce-scatter.12.cloned.1.call-done = f32[32,4096]{1,0:T(8,128)} async-done(((f32[1024,4096]{1,0:T(8,128)}), f32[32,4096]{1,0:T(8,128)}) %reduce-scatter.12.cloned.1.call-update) | async-done | bytes 524304 | tf_op jit(solution)/shard_map/reduce_scatter | solution.py:164
  963.7 187.3 %reduce-scatter.14.cloned.1.call-done = f32[128,1024]{1,0:T(8,128)} async-done(((f32[4096,1024]{1,0:T(8,128)}), f32[128,1024]{1,0:T(8,128)}) %reduce-scatter.14.cloned.1.call-update) | async-done | bytes 524304 | tf_op jit(solution)/shard_map/reduce_scatter | solution.py:165
  (211 shorter events, 151.3 us)
Async XLA Ops:
  7.2 32.2 %copy-start = (bf16[1024,1024]{1,0:T(8,128)(2,1)S(1)}, bf16[1024,1024]{1,0:T(8,128)(2,1)}, u32[]{:S(2)}) copy-start(bf16[1024,1024]{1,0:T(8,128)(2,1)} %param.19) | copy-start | bytes 6291460
  19.9 55.1 %all-to-all-start.1 = ((bf16[4,2,32768]{2,1,0:T(2,128)(2,1)}), bf16[4,2,32768]{2,1,0:T(2,128)(2,1)S(1)}, u32[]{:S(2)}, u32[]{:S(2)}) async-start(bf16[4,2,32768]{2,1,0:T(2,128)(2,1)} %reshape.217), calls=%async_computation.1 | async-start | bytes 1048576 | tf_op jit(solution)/shard_map/all_to_all | solution.py:116
  75.0 64.7 %all-to-all-start.2 = ((bf16[8,640,512]{1,0,2:T(8,128)(2,1)}), bf16[8,640,512]{1,0,2:T(8,128)(2,1)}, u32[]{:S(2)}, u32[]{:S(2)}) async-start(bf16[8,640,512]{1,0,2:T(8,128)(2,1)} %copy.55), calls=%async_computation.2 | async-start | bytes 10485760 | tf_op jit(solution)/shard_map/all_to_all | solution.py:117
  80.3 64.5 %copy-start.47 = (s32[32]{0:T(128)S(1)}, s32[32]{0:T(128)}, u32[]{:S(2)}) copy-start(s32[32]{0:T(128)} %param.17) | copy-start | bytes 388
  139.7 64.5 %all-to-all-start = ((bf16[8,640,512]{1,0,2:T(8,128)(2,1)}), bf16[8,640,512]{1,0,2:T(8,128)(2,1)}, u32[]{:S(2)}, u32[]{:S(2)}) async-start(bf16[8,640,512]{1,0,2:T(8,128)(2,1)} %copy.51), calls=%async_computation | async-start | bytes 10485760 | tf_op jit(solution)/shard_map/all_to_all | solution.py:118
  154.3 56.0 %slice-start.6 = ((s8[5242880]{0:T(1024)(128)(4,1)}), s8[1048576]{0:T(1024)(128)(4,1)S(1)}, s32[]{:S(2)}) async-start(s8[5242880]{0:T(1024)(128)(4,1)} %bitcast.126), calls=%async_computation.24 | async-start | bytes 2097152
  215.9 24.6 %copy-start.4 = (bf16[8,64,1024]{2,1,0:T(8,128)(2,1)S(1)}, bf16[8,64,1024]{2,1,0:T(8,128)(2,1)}, u32[]{:S(2)}) copy-start(bf16[8,64,1024]{2,1,0:T(8,128)(2,1)} %param.16) | copy-start | bytes 3145732
  222.2 20.9 %copy-start.45 = (f32[1024]{0:T(1024)S(1)}, f32[1024]{0:T(1024)}, u32[]{:S(2)}) copy-start(f32[1024]{0:T(1024)} %param.27) | copy-start | bytes 12292
  222.2 20.9 %copy-start.49 = (f32[1024]{0:T(1024)S(1)}, f32[1024]{0:T(1024)}, u32[]{:S(2)}) copy-start(f32[1024]{0:T(1024)} %param.28) | copy-start | bytes 12292
  242.7 51.2 %copy-start.7 = (f32[8,64,1024]{2,1,0:T(8,128)}, f32[8,64,1024]{2,1,0:T(8,128)S(1)}, u32[]{:S(2)}) copy-start(f32[8,64,1024]{2,1,0:T(8,128)S(1)} %get-tuple-element.41) | copy-start | bytes 6291460
  315.3 21.8 %slice-start.8 = ((s8[5242880]{0:T(1024)(128)(4,1)}), s8[1048576]{0:T(1024)(128)(4,1)S(1)}, s32[]{:S(2)}) async-start(s8[5242880]{0:T(1024)(128)(4,1)} %bitcast.129), calls=%async_computation.26 | async-start | bytes 2097152
  342.2 12.9 %all-to-all-start.7 = ((bf16[32,64,128]{2,1,0:T(8,128)(2,1)}), bf16[32,64,128]{2,1,0:T(8,128)(2,1)S(1)}, u32[]{:S(2)}, u32[]{:S(2)}) async-start(bf16[32,64,128]{2,1,0:T(8,128)(2,1)} %copy.67), calls=%async_computation.7 | async-start | bytes 1048576 | tf_op jit(solution)/shard_map/all_to_all | solution.py:144
  355.9 74.5 %all-to-all-start.6 = ((bf16[32,640,128]{1,2,0:T(8,128)(2,1)}), bf16[32,640,128]{1,2,0:T(8,128)(2,1)}, u32[]{:S(2)}, u32[]{:S(2)}) async-start(bf16[32,640,128]{1,2,0:T(8,128)(2,1)} %bitcast.135), calls=%async_computation.6 | async-start | bytes 10485760 | tf_op jit(solution)/shard_map/all_to_all | solution.py:146
  361.1 332.3 %reduce-scatter.10.cloned.1.call-start = ((), (), s32[]{:S(2)}) async-start(), calls=%async_computation.15 | async-start | bytes 2162688 | tf_op jit(solution)/shard_map/reduce_scatter | solution.py:163
  371.0 64.5 %copy-start.16 = (bf16[32,64,128]{2,1,0:T(8,128)(2,1)S(1)}, bf16[32,64,128]{2,1,0:T(8,128)(2,1)}, u32[]{:S(2)}) copy-start(bf16[32,64,128]{2,1,0:T(8,128)(2,1)} %copy-done.15) | copy-start | bytes 1572868
  430.4 74.8 %all-to-all-start.5 = ((bf16[32,640,128]{1,2,0:T(8,128)(2,1)}), bf16[32,640,128]{1,2,0:T(8,128)(2,1)}, u32[]{:S(2)}, u32[]{:S(2)}) async-start(bf16[32,640,128]{1,2,0:T(8,128)(2,1)} %bitcast.134), calls=%async_computation.5 | async-start | bytes 10485760 | tf_op jit(solution)/shard_map/all_to_all | solution.py:145
  435.4 257.9 %reduce-scatter.6.cloned.1.call-start = ((), (), s32[]{:S(2)}) async-start(), calls=%async_computation.13 | async-start | bytes 2162688 | tf_op jit(solution)/shard_map/reduce_scatter | solution.py:161
  439.7 342.3 %reduce-scatter.8.cloned.1.call-start = ((), (), s32[]{:S(2)}) async-start(), calls=%async_computation.14 | async-start | bytes 4325376 | tf_op jit(solution)/shard_map/reduce_scatter | solution.py:162
  549.6 414.1 %reduce-scatter.12.cloned.1.call-start = ((), (), s32[]{:S(2)}) async-start(), calls=%async_computation.16 | async-start | bytes 17301504 | tf_op jit(solution)/shard_map/reduce_scatter | solution.py:164
  563.1 587.9 %reduce-scatter.14.cloned.1.call-start = ((), (), s32[]{:S(2)}) async-start(), calls=%async_computation.17 | async-start | bytes 17301504 | tf_op jit(solution)/shard_map/reduce_scatter | solution.py:165
  574.9 31.5 %slice-start = ((s8[9437184]{0:T(1024)(128)(4,1)}), s8[4194304]{0:T(1024)(128)(4,1)S(1)}, s32[]{:S(2)}) async-start(s8[9437184]{0:T(1024)(128)(4,1)} %bitcast.122), calls=%async_computation.18 | async-start | bytes 8388608
  585.7 18.0 %copy-start.5 = (bf16[8,64,1024]{2,1,0:T(8,128)(2,1)S(1)}, bf16[8,64,1024]{2,1,0:T(8,128)(2,1)}, u32[]{:S(2)}) copy-start(bf16[8,64,1024]{2,1,0:T(8,128)(2,1)} %param.16) | copy-start | bytes 3145732
  585.7 18.0 %copy-start.27 = (bf16[8,64,512]{2,1,0:T(8,128)(2,1)S(1)}, bf16[8,64,512]{2,1,0:T(8,128)(2,1)}, u32[]{:S(2)}) copy-start(bf16[8,64,512]{2,1,0:T(8,128)(2,1)} %copy-done.26) | copy-start | bytes 1572868
  585.7 18.0 %copy-start.33 = (f32[8,64]{1,0:T(8,128)S(1)}, f32[8,64]{1,0:T(8,128)}, u32[]{:S(2)}) copy-start(f32[8,64]{1,0:T(8,128)} %copy-done.32) | copy-start | bytes 6148
  585.7 18.0 %copy-start.38 = (f32[1024]{0:T(1024)S(1)}, f32[1024]{0:T(1024)}, u32[]{:S(2)}) copy-start(f32[1024]{0:T(1024)} %param.25) | copy-start | bytes 12292
  585.7 18.0 %copy-start.48 = (bf16[1024,512]{1,0:T(8,128)(2,1)S(1)}, bf16[1024,512]{1,0:T(8,128)(2,1)}, u32[]{:S(2)}) copy-start(bf16[1024,512]{1,0:T(8,128)(2,1)} %param.18) | copy-start | bytes 3145732
  585.8 20.6 %copy-start.42 = (f32[8,64]{1,0:T(8,128)S(1)}, f32[8,64]{1,0:T(8,128)}, u32[]{:S(2)}) copy-start(f32[8,64]{1,0:T(8,128)} %copy-done.41) | copy-start | bytes 6148
  585.8 20.7 %slice-start.1 = ((s8[9437184]{0:T(1024)(128)(4,1)}), s8[4194304]{0:T(1024)(128)(4,1)S(1)}, s32[]{:S(2)}) async-start(s8[9437184]{0:T(1024)(128)(4,1)} %bitcast.122), calls=%async_computation.19 | async-start | bytes 8388608
  585.8 20.7 %slice-start.2 = ((s8[9437184]{0:T(1024)(128)(4,1)}), s8[1048576]{0:T(1024)(128)(4,1)S(1)}, s32[]{:S(2)}) async-start(s8[9437184]{0:T(1024)(128)(4,1)} %bitcast.122), calls=%async_computation.20 | async-start | bytes 2097152
  585.8 20.7 %copy-start.25 = (f32[8,576]{1,0:T(8,128)S(1)}, f32[8,576]{1,0:T(8,128)}, u32[]{:S(2)}) copy-start(f32[8,576]{1,0:T(8,128)} %copy-done.24) | copy-start | bytes 55300
  585.8 20.7 %copy-start.37 = (f32[1024]{0:T(1024)S(1)}, f32[1024]{0:T(1024)}, u32[]{:S(2)}) copy-start(f32[1024]{0:T(1024)} %param.23) | copy-start | bytes 12292
  616.7 57.5 %copy-start.40 = (f32[8,64]{1,0:T(8,128)S(1)}, f32[8,64]{1,0:T(8,128)}, u32[]{:S(2)}) copy-start(f32[8,64]{1,0:T(8,128)} %copy-done.39) | copy-start | bytes 6148
  (41 other events, 302.9 us)
Sparse Core Ops, SparseCore 0:
  364.8 141.8 reduce-scatter.9
  509.6 132.6 reduce-scatter.5
  645.1 136.8 reduce-scatter.7
  784.7 178.8 reduce-scatter.11
  966.4 184.5 reduce-scatter.13
where the time goes:
time: 1160 us
  waiting for transfers between devices  664 us (57%)
  matrix products  174 us (15%)
  local copies, waits for them, and re-layouts  117 us (10%)
  other arithmetic  91.9 us (8%)
  blocking collectives  66.6 us (6%)
  starting transfers between devices  28.8 us (2%)
  between operations  14.9 us (1%)
    reduce_scatter x1, waiting for transfers between devices, on_device(): lax.psum_scatter(grad_outer, ('img', 'head'), scatter_dimension=0, tiled=...  187 us
    reduce_scatter x1, waiting for transfers between devices, on_device(): lax.psum_scatter(grad_inner, ('img', 'head'), scatter_dimension=0, tiled=...  182 us
    reduce_scatter x1, waiting for transfers between devices, on_device(): lax.psum_scatter(grad_keyval, ('img', 'head'), scatter_dimension=0, tiled...  88.7 us
    all_to_all x1, waiting for transfers between devices, on_device(): lax.all_to_all(value_grad, 'head', split_axis=0, concat_axis=2, tiled=True)  59.3 us
    all_to_all x1, waiting for transfers between devices, on_device(): lax.all_to_all(key_rows, 'head', split_axis=2, concat_axis=0, tiled=True)  50.2 us
    all_to_all x1, waiting for transfers between devices, on_device(): lax.all_to_all(value_rows, 'head', split_axis=2, concat_axis=0, tiled=True)  50 us
    dot_general x5, matrix products, outer_product(): jnp.einsum('ind,ine->de', left_rows, right_rows, preferred_element_type=j...  48.9 us
    all_to_all x1, waiting for transfers between devices, on_device(): lax.all_to_all(key_grad, 'head', split_axis=0, concat_axis=2, tiled=True)  47.1 us
  transfers between devices with their start and end apart: 11, of which 7 were waited for; matrix products, arithmetic and copies ran while one was open for 21% of the time, Pallas kernels for 0%

commit v1 on v0

v1 whole, which is shorter than its diff:
```python
import functools

import jax
import jax.numpy as jnp
from jax import lax
from jax.experimental import pallas as pl
from jax.experimental.pallas import tpu as pltpu
from jax.sharding import PartitionSpec as P

HEAD_DIM = 64
GROUP = 256
norm_eps = 1e-05
masked_score = -1e30
both = ("img", "head")
bf16, f32 = jnp.bfloat16, jnp.float32
VMEM_LIMIT = 56 << 20


def shape(dims, dtype):
    return jax.ShapeDtypeStruct(dims, dtype)


def dot(left, right, left_dim=1, right_dim=0):
    return lax.dot_general(
        left, right, (((left_dim,), (right_dim,)), ((), ())), preferred_element_type=f32
    )


def call(body, flops, bytes_accessed, **kwargs):
    return pl.pallas_call(
        body,
        compiler_params=pltpu.CompilerParams(vmem_limit_bytes=VMEM_LIMIT),
        cost_estimate=pl.CostEstimate(
            flops=flops, bytes_accessed=bytes_accessed, transcendentals=0
        ),
        **kwargs,
    )


def normalise(values):
    centre = values - jnp.mean(values, axis=-1, keepdims=True)
    spread = jnp.mean(centre * centre, axis=-1, keepdims=True)
    factor = lax.rsqrt(spread + norm_eps)
    return centre * factor, factor


def norm_back(grad, normed, factor, gain):
    scaled = grad * gain
    average = jnp.mean(scaled, axis=-1, keepdims=True)
    along = jnp.mean(scaled * normed, axis=-1, keepdims=True)
    return factor * (scaled - average - normed * along)


def own_head():
    row = lax.broadcasted_iota(jnp.int32, (GROUP, GROUP), 0) // HEAD_DIM
    column = lax.broadcasted_iota(jnp.int32, (GROUP, GROUP), 1) // HEAD_DIM
    return row == column


def stack_heads(rows, own):
    repeated = jnp.concatenate([rows.astype(f32)] * (GROUP // HEAD_DIM), axis=0)
    return jnp.where(own, repeated, 0.0).astype(bf16)


def unstack_heads(full, own):
    full = jnp.where(own, full, 0.0)
    rows = full.shape[0] // (GROUP // HEAD_DIM)
    return sum(full[h * rows : (h + 1) * rows] for h in range(GROUP // HEAD_DIM))


def score_columns(key_group, stacked, length, media_rows):
    scores = dot(key_group, stacked, 1, 1)
    position = lax.broadcasted_iota(jnp.int32, scores.shape, 0)
    usable = (position < length) | (position >= media_rows)
    return jnp.where(usable, scores, masked_score)


def attend_body(
    lengths, media, latents, query_weight, keyval_weight, media_gain, media_bias,
    latent_gain, latent_bias, keyval_in, keyval, query, mixed, log_total,
):
    per_step, media_rows, width = media.shape
    latent_rows = latents.shape[1]
    inner = query_weight.shape[1]
    own = own_head()
    for i in range(per_step):
        normed, _ = normalise(media[i].astype(f32))
        keyval_in[i, :media_rows] = (normed * media_gain[...] + media_bias[...]).astype(bf16)
        normed, _ = normalise(latents[i].astype(f32))
        latent_low = (normed * latent_gain[...] + latent_bias[...]).astype(bf16)
        keyval_in[i, media_rows:] = latent_low
        query[i] = (dot(latent_low, query_weight[...]) * 0.125).astype(bf16)
        keyval[i] = dot(keyval_in[i], keyval_weight[...]).astype(bf16)
        length = lengths[pl.program_id(0) * per_step + i]
        for g in range(inner // GROUP):
            at = pl.ds(g * GROUP, GROUP)
            stacked = stack_heads(query[i, :, at], own)
            scores = score_columns(keyval[i, :, at], stacked, length, media_rows)
            top = jnp.max(scores, axis=0, keepdims=True)
            exps = jnp.exp(scores - top)
            total = jnp.sum(exps, axis=0, keepdims=True)
            log_total[i, :, at] = top + jnp.log(total)
            prob_low = (exps * (1.0 / total)).astype(bf16)
            full = dot(prob_low, keyval[i, :, pl.ds(inner + g * GROUP, GROUP)], 0, 0)
            mixed[i, :, at] = unstack_heads(full, own).astype(bf16)


def attend(lengths, media, latents, query_weight, keyval_weight, gains, per_step=1):
    images, media_rows, width = media.shape
    latent_rows = latents.shape[1]
    inner = query_weight.shape[1]
    keys = media_rows + latent_rows

    def rows(count, columns):
        return pl.BlockSpec((per_step, count, columns), lambda i, _: (i, 0, 0))

    def whole(*dims):
        return pl.BlockSpec(dims, lambda i, _: (0,) * len(dims))

    vector = whole(1, width)
    return call(
        attend_body,
        2 * images * keys * width * 2 * inner * 13 // 10,
        images * (media_rows * width * 2 + 2 * keys * width * 2),
        grid_spec=pltpu.PrefetchScalarGridSpec(
            num_scalar_prefetch=1,
            grid=(images // per_step,),
            in_specs=[
                rows(media_rows, width), rows(latent_rows, width), whole(width, inner),
                whole(width, 2 * inner), vector, vector, vector, vector,
            ],
            out_specs=[
                rows(keys, width), rows(keys, 2 * inner), rows(latent_rows, inner),
                rows(latent_rows, inner), rows(1, inner),
            ],
        ),
        out_shape=[
            shape((images, keys, width), bf16),
            shape((images, keys, 2 * inner), bf16),
            shape((images, latent_rows, inner), bf16),
            shape((images, latent_rows, inner), bf16),
            shape((images, 1, inner), f32),
        ],
    )(lengths, media, latents, query_weight, keyval_weight, *gains)


def split_rows(source, keep, send, mine, shards):
    size = source.shape[0] // shards
    low = jnp.bitwise_and(mine, shards - 1)
    for k in range(shards // 2):
        for target, place in ((keep, 2 * k), (send, 2 * k + 1)):
            at = pl.multiple_of(jnp.bitwise_xor(low, place) * size, size)
            target[pl.ds(k * size, size), :] = source[pl.ds(at, size), :]


def erf_parts(values):
    z = jnp.abs(values) * (0.5 ** 0.5)
    t = 1.0 / (1.0 + 0.3275911 * z)
    density = jnp.exp(-z * z)
    tail = t * (0.127414796 + t * (-0.142248368 + t * (0.7107068705 + t * (-0.7265760135 + t * 0.5307027145))))
    tail = tail * density
    return jnp.where(values < 0, tail, 1.0 - tail), density * 0.3989422804014327


def feed_body(
    shards, mine, mixed, latents, output_weight, feed_gain, feed_bias, cotangent, inner_weight,
    outer_weight, residual, hidden_keep, hidden_send, activation, inner_grad, hidden, turned,
):
    @pl.when(pl.program_id(0) == 0)
    def _():
        residual[...] = latents[...].astype(f32) + dot(mixed[...], output_weight[...])
        normed, _ = normalise(residual[...])
        low = (normed * feed_gain[...] + feed_bias[...])
        hidden[...] = low.astype(bf16)
        turned[...] = jnp.transpose(low).astype(bf16)
        split_rows(turned, hidden_keep, hidden_send, mine[0], shards)

    inner_rows = dot(hidden[...], inner_weight[...])
    below, density = erf_parts(inner_rows)
    activation[...] = (inner_rows * below).astype(bf16)
    activation_grad = dot(cotangent[...], outer_weight[...], 1, 1)
    inner_grad[...] = (activation_grad * (below + inner_rows * density)).astype(bf16)


def feed(mine, shards, mixed, latents, output_weight, feed_gain, feed_bias, cotangent,
         inner_weight, outer_weight, tile=512):
    rows, width = latents.shape
    inner = mixed.shape[1]
    hidden_units = inner_weight.shape[1]

    def whole(*dims):
        return pl.BlockSpec(dims, lambda t, _: (0,) * len(dims))

    return call(
        functools.partial(feed_body, shards),
        4 * rows * width * hidden_units,
        4 * width * hidden_units + 4 * rows * hidden_units,
        grid_spec=pltpu.PrefetchScalarGridSpec(
            num_scalar_prefetch=1,
            grid=(hidden_units // tile,),
            in_specs=[
                whole(rows, inner), whole(rows, width), whole(inner, width), whole(1, width),
                whole(1, width), whole(rows, width),
                pl.BlockSpec((width, tile), lambda t, _: (0, t)),
                pl.BlockSpec((tile, width), lambda t, _: (t, 0)),
            ],
            out_specs=[
                whole(rows, width), whole(width // 2, rows), whole(width // 2, rows),
                pl.BlockSpec((rows, tile), lambda t, _: (0, t)),
                pl.BlockSpec((rows, tile), lambda t, _: (0, t)),
            ],
            scratch_shapes=[pltpu.VMEM((rows, width), bf16), pltpu.VMEM((width, rows), bf16)],
        ),
        out_shape=[
            shape((rows, width), f32), shape((width // 2, rows), bf16),
            shape((width // 2, rows), bf16), shape((rows, hidden_units), bf16),
            shape((rows, hidden_units), bf16),
        ],
    )(mine, mixed, latents, output_weight, feed_gain, feed_bias, cotangent, inner_weight, outer_weight)


def outer_grad_body(shards, mine, activation, cotangent, keep, send, product):
    product[...] = dot(activation[...], cotangent[...], 0, 0).astype(bf16)
    split_rows(product, keep, send, mine[0], shards)


def outer_grad(mine, shards, activation, cotangent, half, halves, tile=1024):
    rows, hidden_units = activation.shape
    columns = cotangent.shape[1] // halves
    group = shards * tile // hidden_units
    place = pl.BlockSpec(
        (tile // 2, columns), lambda t, mine: (jnp.bitwise_xor(t, mine[0] // group), 0)
    )
    return call(
        functools.partial(outer_grad_body, group),
        2 * rows * hidden_units * columns,
        2 * hidden_units * (rows + columns),
        grid_spec=pltpu.PrefetchScalarGridSpec(
            num_scalar_prefetch=1,
            grid=(hidden_units // tile,),
            in_specs=[
                pl.BlockSpec((rows, tile), lambda t, _: (0, t)),
                pl.BlockSpec((rows, columns), lambda t, _: (0, half)),
            ],
            out_specs=[place, place],
            scratch_shapes=[pltpu.VMEM((tile, columns), bf16)],
        ),
        out_shape=[shape((hidden_units // 2, columns), bf16)] * 2,
    )(mine, activation, cotangent)


def inner_grad_body(hidden_keep, hidden_send, inner_grad, keep, send):
    send[...] = dot(hidden_send[...], inner_grad[...]).astype(bf16)
    keep[...] = dot(hidden_keep[...], inner_grad[...]).astype(bf16)


def inner_weight_grad(hidden_keep, hidden_send, inner_grad, half, halves, tile=512):
    held, rows = hidden_keep.shape
    columns = inner_grad.shape[1] // halves
    steps = columns // tile
    whole = pl.BlockSpec((held, rows), lambda t: (0, 0))
    place = pl.BlockSpec((held, tile), lambda t: (0, t))
    return call(
        inner_grad_body,
        4 * rows * held * columns,
        2 * columns * (rows + 2 * held),
        grid=(steps,),
        in_specs=[whole, whole, pl.BlockSpec((rows, tile), lambda t: (0, half * steps + t))],
        out_specs=[place, place],
        out_shape=[shape((held, columns), bf16)] * 2,
    )(hidden_keep, hidden_send, inner_grad)


def feed_back_body(
    shards, mine, inner_grad, inner_weight, residual, feed_gain, cotangent, mixed, output_weight,
    residual_grad, mixed_grad, keep, send, sums, total, product,
):
    step = pl.program_id(0)
    part = dot(inner_grad[...], inner_weight[...], 1, 1)

    @pl.when(step == 0)
    def _():
        total[...] = part

    @pl.when(step > 0)
    def _():
        total[...] += part

    @pl.when(step == pl.num_programs(0) - 1)
    def _():
        hidden_grad = total[...]
        normed, factor = normalise(residual[...])
        sums[...] = jnp.concatenate(
            [
                jnp.sum(hidden_grad * normed, axis=0, keepdims=True),
                jnp.sum(hidden_grad, axis=0, keepdims=True),
                jnp.zeros((6, hidden_grad.shape[1]), f32),
            ],
            axis=0,
        )
        grad = cotangent[...].astype(f32) + norm_back(hidden_grad, normed, factor, feed_gain[...])
        residual_grad[...] = grad
        low = grad.astype(bf16)
        mixed_grad[...] = dot(low, output_weight[...], 1, 1).astype(bf16)
        product[...] = dot(mixed[...], low, 0, 0).astype(bf16)
        split_rows(product, keep, send, mine[0], shards)


def feed_back(mine, shards, inner_grad, inner_weight, residual, feed_gain, cotangent, mixed,
              output_weight, tile=1024):
    rows, hidden_units = inner_grad.shape
    width = inner_weight.shape[0]
    inner = mixed.shape[1]

    def whole(*dims):
        return pl.BlockSpec(dims, lambda t, _: (0,) * len(dims))

    return call(
        functools.partial(feed_back_body, shards),
        2 * rows * width * hidden_units + 4 * rows * width * inner,
        2 * hidden_units * (rows + width) + 8 * rows * width,
        grid_spec=pltpu.PrefetchScalarGridSpec(
            num_scalar_prefetch=1,
            grid=(hidden_units // tile,),
            in_specs=[
                pl.BlockSpec((rows, tile), lambda t, _: (0, t)),
                pl.BlockSpec((width, tile), lambda t, _: (0, t)),
                whole(rows, width), whole(1, width), whole(rows, width), whole(rows, inner),
                whole(inner, width),
            ],
            out_specs=[
                whole(rows, width), whole(rows, inner), whole(inner // 2, width),
                whole(inner // 2, width), whole(8, width),
            ],
            scratch_shapes=[pltpu.VMEM((rows, width), f32), pltpu.VMEM((inner, width), bf16)],
        ),
        out_shape=[
            shape((rows, width), f32), shape((rows, inner), bf16), shape((inner // 2, width), bf16),
            shape((inner // 2, width), bf16), shape((8, width), f32),
        ],
    )(mine, inner_grad, inner_weight, residual, feed_gain, cotangent, mixed, output_weight)


def result_body(activation, outer_weight, residual, result, total):
    step = pl.program_id(0)
    part = dot(activation[...], outer_weight[...])

    @pl.when(step == 0)
    def _():
        total[...] = residual[...] + part

    @pl.when(step > 0)
    def _():
        total[...] += part

    @pl.when(step == pl.num_programs(0) - 1)
    def _():
        result[...] = total[...].astype(bf16)


def result_rows(activation, outer_weight, residual, tile=1024):
    rows, hidden_units = activation.shape
    width = outer_weight.shape[1]
    whole = pl.BlockSpec((rows, width), lambda t: (0, 0))
    return call(
        result_body,
        2 * rows * width * hidden_units,
        2 * hidden_units * (rows + width) + 6 * rows * width,
        grid=(hidden_units // tile,),
        in_specs=[
            pl.BlockSpec((rows, tile), lambda t: (0, t)),
            pl.BlockSpec((tile, width), lambda t: (t, 0)),
            whole,
        ],
        out_specs=whole,
        out_shape=shape((rows, width), bf16),
        scratch_shapes=[pltpu.VMEM((rows, width), f32)],
    )(activation, outer_weight, residual)


def attend_back_body(
    shards, media_rows, lengths, mine, keyval_in, keyval, query, mixed_grad, log_total, feed_sums,
    query_weight, keyval_weight, norms, keyval_grad, query_grad, keyval_keep, keyval_send,
    query_keep, query_send, sums_keep, sums_send, media_total, latent_in, latent_grad, latent_query,
    sum_rows, keyval_product, query_product, sum_product,
):
    step = pl.program_id(0)
    per_step, keys, width = keyval_in.shape
    latent_rows = keys - media_rows
    inner = query.shape[2]
    own = own_head()

    @pl.when(step == 0)
    def _():
        media_total[...] = jnp.zeros_like(media_total)
        sum_rows[...] = jnp.zeros_like(sum_rows)

    for i in range(per_step):
        length = lengths[step * per_step + i]
        for g in range(inner // GROUP):
            at = pl.ds(g * GROUP, GROUP)
            value_at = pl.ds(inner + g * GROUP, GROUP)
            stacked = stack_heads(query[i, :, at], own)
            scores = score_columns(keyval[i, :, at], stacked, length, media_rows)
            prob_rows = jnp.exp(scores - log_total[i, :, at])
            stacked_grad = stack_heads(mixed_grad[i, :, at], own)
            prob_grad = dot(keyval[i, :, value_at], stacked_grad, 1, 1)
            value_grad = dot(prob_rows.astype(bf16), stacked_grad).astype(bf16)
            keyval_grad[i, :, value_at] = value_grad
            along = jnp.sum(prob_rows * prob_grad, axis=0, keepdims=True)
            score_grad = (prob_rows * (prob_grad - along)).astype(bf16)
            keyval_grad[i, :, at] = dot(score_grad, stacked).astype(bf16)
            full = dot(score_grad, keyval[i, :, at], 0, 0)
            query_grad[i, :, at] = unstack_heads(full, own).astype(bf16)
        media_total[...] += dot(keyval_in[i, :media_rows], keyval_grad[i, :media_rows], 0, 0)
        sum_rows[0:1, :] += jnp.sum(keyval_grad[i, :media_rows].astype(f32), axis=0, keepdims=True)
        at = pl.ds(pl.multiple_of((step * per_step + i) * latent_rows, latent_rows), latent_rows)
        latent_in[at, :] = keyval_in[i, media_rows:]
        latent_grad[at, :] = keyval_grad[i, media_rows:]
        latent_query[at, :] = query_grad[i]

    @pl.when(step == pl.num_programs(0) - 1)
    def _():
        latent_total = dot(latent_in[...], latent_grad[...], 0, 0)
        query_total = dot(latent_in[...], latent_query[...], 0, 0) * 0.125
        keyval_product[...] = (media_total[...] + latent_total).astype(bf16)
        query_product[...] = query_total.astype(bf16)
        keyval_rows = keyval_weight[...].astype(f32)
        query_rows = query_weight[...].astype(f32)
        latent_sum = jnp.sum(latent_grad[...].astype(f32), axis=0, keepdims=True)
        query_sum = jnp.sum(latent_query[...].astype(f32), axis=0, keepdims=True) * 0.125

        def along(values):
            return jnp.sum(values, axis=1, keepdims=True)

        columns = norms[...]
        media_gain, media_bias = columns[:, 0:1], columns[:, 1:2]
        latent_gain, latent_bias = columns[:, 2:3], columns[:, 3:4]
        media_bias_grad = along(keyval_rows * sum_rows[0:1, :])
        media_gain_grad = (
            along(keyval_rows * media_total[...]) - media_bias * media_bias_grad
        ) / media_gain
        latent_bias_grad = along(keyval_rows * latent_sum) + along(query_rows * query_sum)
        latent_gain_grad = (
            along(keyval_rows * latent_total) + along(query_rows * query_total)
            - latent_bias * latent_bias_grad
        ) / latent_gain
        feed_columns = jnp.transpose(
            jnp.concatenate([feed_sums[...], jnp.zeros((120, width), f32)], axis=0)
        )
        lane = lax.broadcasted_iota(jnp.int32, (width, 128), 1)
        packed = jnp.where(lane == 0, media_gain_grad, 0.0)
        packed = jnp.where(lane == 1, media_bias_grad, packed)
        packed = jnp.where(lane == 2, latent_gain_grad, packed)
        packed = jnp.where(lane == 3, latent_bias_grad, packed)
        packed = jnp.where(lane == 4, feed_columns[:, 0:1], packed)
        packed = jnp.where(lane == 5, feed_columns[:, 1:2], packed)
        sum_product[...] = packed
        split_rows(keyval_product, keyval_keep, keyval_send, mine[0], shards)
        split_rows(query_product, query_keep, query_send, mine[0], shards)
        split_rows(sum_product, sums_keep, sums_send, mine[0], shards)


def attend_back(mine, shards, media_rows, lengths, keyval_in, keyval, query, mixed_grad, log_total,
                feed_sums, query_weight, keyval_weight, norms, per_step=2):
    images, keys, width = keyval_in.shape
    latent_rows = keys - media_rows
    inner = query.shape[2]
    latents = images * latent_rows

    def rows(count, columns):
        return pl.BlockSpec((per_step, count, columns), lambda i, *_: (i, 0, 0))

    def whole(*dims):
        return pl.BlockSpec(dims, lambda i, *_: (0,) * len(dims))

    half = width // 2
    halves = [(half, 2 * inner, bf16), (half, inner, bf16), (half, 128, f32)]
    halves = [h for h in halves for _ in range(2)]
    return call(
        functools.partial(attend_back_body, shards, media_rows),
        2 * images * keys * width * 2 * inner * 15 // 10,
        6 * images * keys * width,
        grid_spec=pltpu.PrefetchScalarGridSpec(
            num_scalar_prefetch=2,
            grid=(images // per_step,),
            in_specs=[
                rows(keys, width), rows(keys, 2 * inner), rows(latent_rows, inner),
                rows(latent_rows, inner), rows(1, inner), whole(8, width), whole(width, inner),
                whole(width, 2 * inner), whole(width, 4),
            ],
            out_specs=[rows(keys, 2 * inner), rows(latent_rows, inner)]
            + [whole(h[0], h[1]) for h in halves],
            scratch_shapes=[
                pltpu.VMEM((width, 2 * inner), f32), pltpu.VMEM((latents, width), bf16),
                pltpu.VMEM((latents, 2 * inner), bf16), pltpu.VMEM((latents, inner), bf16),
                pltpu.VMEM((8, 2 * inner), f32), pltpu.VMEM((width, 2 * inner), bf16),
                pltpu.VMEM((width, inner), bf16), pltpu.VMEM((width, 128), f32),
            ],
        ),
        out_shape=[
            shape((images, keys, 2 * inner), bf16), shape((images, latent_rows, inner), bf16),
        ] + [shape(h[:2], h[2]) for h in halves],
    )(lengths, mine, keyval_in, keyval, query, mixed_grad, log_total, feed_sums, query_weight,
      keyval_weight, norms)


def input_grad_body(
    media, latents, keyval_grad, query_grad, residual_grad, query_weight, keyval_weight,
    media_gain, latent_gain, grad_media, grad_latents,
):
    per_step, media_rows, width = media.shape
    for i in range(per_step):
        norm_grad = dot(keyval_grad[i, :media_rows], keyval_weight[...], 1, 1)
        normed, factor = normalise(media[i].astype(f32))
        grad_media[i] = norm_back(norm_grad, normed, factor, media_gain[...]).astype(bf16)
        norm_grad = dot(keyval_grad[i, media_rows:], keyval_weight[...], 1, 1)
        norm_grad += dot(query_grad[i], query_weight[...], 1, 1) * 0.125
        normed, factor = normalise(latents[i].astype(f32))
        part = norm_back(norm_grad, normed, factor, latent_gain[...])
        grad_latents[i] = (residual_grad[i] + part).astype(bf16)


def input_grad(media, latents, keyval_grad, query_grad, residual_grad, query_weight, keyval_weight,
               media_gain, latent_gain, per_step=1):
    images, media_rows, width = media.shape
    latent_rows = latents.shape[1]
    inner = query_weight.shape[1]
    keys = media_rows + latent_rows

    def rows(count, columns):
        return pl.BlockSpec((per_step, count, columns), lambda i: (i, 0, 0))

    def whole(*dims):
        return pl.BlockSpec(dims, lambda i: (0,) * len(dims))

    return call(
        input_grad_body,
        2 * images * keys * width * 2 * inner * 12 // 10,
        6 * images * keys * width,
        grid=(images // per_step,),
        in_specs=[
            rows(media_rows, width), rows(latent_rows, width), rows(keys, 2 * inner),
            rows(latent_rows, inner), rows(latent_rows, width), whole(width, inner),
            whole(width, 2 * inner), whole(1, width), whole(1, width),
        ],
        out_specs=[rows(media_rows, width), rows(latent_rows, width)],
        out_shape=[shape(media.shape, bf16), shape(latents.shape, bf16)],
    )(media, latents, keyval_grad, query_grad, residual_grad, query_weight, keyval_weight,
      media_gain, latent_gain)


def swap(values, bit, devices):
    pairs = [(d, d ^ (1 << bit)) for d in range(devices)]
    return lax.ppermute(values, both, pairs)


def add(left, right, dtype):
    return (left.astype(f32) + right.astype(f32)).astype(dtype)


def share_of_sum(keep, send, devices, order):
    kind = keep.dtype
    bits = devices.bit_length() - 1
    rows, columns = keep.shape[0] // (devices // 2), keep.shape[1]
    left = list(range(bits - 1, 0, -1))
    keep = keep.reshape([2] * (bits - 1) + [rows, columns])
    got = swap(send, 0, devices).reshape(keep.shape)
    for step, bit in enumerate(order):
        axis = left.index(bit)
        left.remove(bit)
        lower = functools.partial(lax.index_in_dim, index=0, axis=axis, keepdims=False)
        upper = functools.partial(lax.index_in_dim, index=1, axis=axis, keepdims=False)
        send = add(upper(keep), upper(got), kind)
        keep = add(lower(keep), lower(got), kind)
        got = swap(send, bit, devices)
    return add(keep, got, f32)


def natural_share(keep, send, shards):
    rows, columns = keep.shape[0] // (shards // 2), keep.shape[1]
    parts = [v.reshape(shards // 2, rows, columns).astype(f32) for v in (keep, send)]
    return lax.psum_scatter(
        jnp.stack(parts, axis=1).reshape(-1, columns), both, scatter_dimension=0, tiled=True
    )


def on_device(
    devices, heads, media_tokens, latents, lengths, query_weight, keyval_weight, output_weight,
    inner_weight, outer_weight, media_gain, media_bias, latent_gain, latent_bias, feed_gain,
    feed_bias, cotangent,
):
    images, media_rows, width = media_tokens.shape
    latent_rows = latents.shape[1]
    inner = query_weight.shape[1]
    thin = devices > inner // 16 or devices < 4
    shards = 32 if thin else devices
    own = lax.axis_index(both)
    mine = jnp.zeros((1,), jnp.int32) if thin else own.reshape(1).astype(jnp.int32)
    own_lengths = lax.dynamic_slice_in_dim(lengths, lax.axis_index("head") * images, images)
    row = lambda v: v.reshape(1, width)
    flat = lambda v: v.reshape(images * latent_rows, v.shape[2])
    deep = lambda v: v.reshape(images, latent_rows, v.shape[1])

    norms = (row(media_gain), row(media_bias), row(latent_gain), row(latent_bias))
    keyval_in, keyval, query, mixed, log_total = attend(
        own_lengths, media_tokens, latents, query_weight, keyval_weight, norms
    )
    flat_mixed, flat_cotangent = flat(mixed), flat(cotangent)
    residual, hidden_keep, hidden_send, activation, inner_grad = feed(
        mine, shards, flat_mixed, flat(latents), output_weight, row(feed_gain), row(feed_bias),
        flat_cotangent, inner_weight, outer_weight,
    )
    outer_parts = [outer_grad(mine, shards, activation, flat_cotangent, h, 2) for h in range(2)]
    inner_parts = [inner_weight_grad(hidden_keep, hidden_send, inner_grad, h, 2) for h in range(2)]
    residual_grad, mixed_grad, output_keep, output_send, feed_sums = feed_back(
        mine, shards, inner_grad, inner_weight, residual, row(feed_gain), flat_cotangent,
        flat_mixed, output_weight,
    )
    columns = jnp.stack([media_gain, media_bias, latent_gain, latent_bias], axis=1)
    back = attend_back(
        mine, shards, media_rows, own_lengths, keyval_in, keyval, query, deep(mixed_grad),
        log_total, feed_sums, query_weight, keyval_weight, columns,
    )
    keyval_grad, query_grad = back[:2]
    grad_media, grad_latents = input_grad(
        media_tokens, latents, keyval_grad, query_grad, deep(residual_grad), query_weight,
        keyval_weight, row(media_gain), row(latent_gain),
    )
    out_latents = deep(result_rows(activation, outer_weight, residual))

    if thin:
        share = lambda pair, first: natural_share(*pair, shards)
    else:
        bits = devices.bit_length() - 1
        along = [[2, 1] + list(range(3, bits)), [1, 2] + list(range(3, bits))] if bits > 2 else [[1], [1]]
        share = lambda pair, first: share_of_sum(*pair, devices, along[first])

    grad_outer = jnp.concatenate([share(outer_parts[h], h) for h in range(2)], axis=1)
    grad_inner = jnp.concatenate([share(inner_parts[h], h) for h in range(2)], axis=1)
    grad_output = share((output_keep, output_send), 1)
    grad_keyval = share(back[2:4], 0)
    grad_query = share(back[4:6], 1)
    sums = share(back[6:8], 1)
    return (
        out_latents, grad_media, grad_latents, grad_query, grad_keyval, grad_output, grad_inner,
        grad_outer, sums[:, 0], sums[:, 1], sums[:, 2], sums[:, 3], sums[:, 4], sums[:, 5],
    )


def solution(mesh):
    spread = P(both, None, None)
    return jax.shard_map(
        functools.partial(on_device, mesh.size, mesh.shape["head"]),
        mesh=mesh,
        in_specs=(spread, spread, P("img")) + (P(),) * 11 + (spread,),
        out_specs=(spread,) * 3 + (P(both, None),) * 5 + (P(both),) * 6,
        check_vma=False,
    )
```

time: 1160 us -> 395 us (0.34)
  waiting for transfers between devices: 664 us -> 121 us
  Pallas kernels: 0 us -> 177 us
  matrix products: 174 us -> 0 us
  local copies, waits for them, and re-layouts: 117 us -> 25.3 us
  other arithmetic: 91.9 us -> 13.2 us
  blocking collectives: 66.6 us -> 0 us
  starting transfers between devices: 28.8 us -> 54.9 us
  between operations: 14.9 us -> 1.29 us
    reduce_scatter x5 -> x0, waiting for transfers between devices: 458 us -> none  [the longest x1 187 us: on_device(): lax.psum_scatter(grad_outer, ('img', 'head'), scatter_dimension=0, tiled=...]
    all_to_all x6 -> x0, waiting for transfers between devices: 207 us -> none  [the longest x1 59.3 us: on_device(): lax.all_to_all(value_grad, 'head', split_axis=0, concat_axis=2, tiled=True)]
    pallas_call x0 -> x10, Pallas kernels: none -> 177 us  [the longest x1 37.7 us: attend_back(): call(functools.partial(attend_back_body, shards, media_rows), 2 * images...]
    dot_general x21 -> x0, matrix products: 174 us -> none  [the longest x5 48.9 us: outer_product(): jnp.einsum('ind,ine->de', left_rows, right_rows, preferred_element_type=j...]
    ppermute x0 -> x40, waiting for transfers between devices: none -> 121 us  [swap(): return lax.ppermute(values, both, pairs)]
    ppermute x0 -> x40, starting transfers between devices: none -> 54.9 us  [swap(): return lax.ppermute(values, both, pairs)]
    all_to_all x10 -> x0, local copies, waits for them, and re-layouts: 52.1 us -> none  [the longest x2 18.3 us: on_device(): lax.all_to_all(value_grad, 'head', split_axis=0, concat_axis=2, tiled=True)]
    convert_element_type x7 -> x35, other arithmetic: 53 us -> 5.89 us  [add(): return (left.astype(f32) + right.astype(f32)).astype(dtype)]
  transfers between devices with their start and end apart: 11 -> 40, of which waited for: 7 -> 27; matrix products, arithmetic and copies ran while one was open for 21% -> 7% of each run, Pallas kernels for 0% -> 19%
where the time goes in v1:
time: 395 us; the launch traced here: 392 us
  Pallas kernels  177 us (45%)
  waiting for transfers between devices  121 us (31%)
  starting transfers between devices  54.9 us (14%)
  local copies, waits for them, and re-layouts  25.3 us (6%)
  other arithmetic  13.2 us (3%)
    ppermute x40, waiting for transfers between devices, swap(): return lax.ppermute(values, both, pairs)  121 us
    ppermute x40, starting transfers between devices, swap(): return lax.ppermute(values, both, pairs)  54.9 us
    pallas_call x1, Pallas kernels, attend_back(): call(functools.partial(attend_back_body, shards, media_rows), 2 * images...  37.7 us
    pallas_call x1, Pallas kernels, attend(): call(attend_body, 2 * images * keys * width * 2 * inner * 13 // 10, image...  30.2 us
    pallas_call x1, Pallas kernels, input_grad(): call(input_grad_body, 2 * images * keys * width * 2 * inner * 12 // 10, 6...  29.1 us
    pallas_call x1, Pallas kernels, result_rows(): call(result_body, 2 * rows * width * hidden_units, 2 * hidden_units * (ro...  22.1 us
    pallas_call x1, Pallas kernels, feed(): call(functools.partial(feed_body, shards), 4 * rows * width * hidden_unit...  19.5 us
    pallas_call x1, Pallas kernels, feed_back(): call(functools.partial(feed_back_body, shards), 2 * rows * width * hidden...  14.1 us
  transfers between devices with their start and end apart: 40, of which 27 were waited for; matrix products, arithmetic and copies ran while one was open for 7% of the time, Pallas kernels for 19%

profile of v1, /device:TPU:0, one launch (start us, length us, event | category | flops | bytes accessed | tf_op | source)
XLA Modules:
  0.0 392.5 jit_solution(8522999620488353241)
XLA Ops:
  3.7 30.2 %shard_map.254 = (bf16[8,640,1024]{2,1,0:T(8,128)(2,1)}, bf16[8,640,1024]{2,1,0:T(8,128)(2,1)}, bf16[8,64,512]{2,1,0:T(8,128)(2,1)}, bf16[8,64,512]{2,1,0:T(8,128)(2,1)}, f32[8,1,512]{2,1,0:T(1,128)}) custom-call(s32[8]{0:T(128)} %dynamic_slice.3.lengths, bf16[8,576,1024]{2,1,0:T(8,128)(2,1)} %media.3, bf16[8,64,1024]{2,1,0:T(8,128)(2,1)} %latents.3, ...), custom_call_target="tpu_custom_call" | custom-call | flops 13958643712 | bytes 30408704 | tf_op jit(solution)/shard_map/pallas_call | solution.py:121
  33.8 19.5 %shard_map.255 = (f32[512,1024]{1,0:T(8,128)}, bf16[512,512]{1,0:T(8,128)(2,1)}, bf16[512,512]{1,0:T(8,128)(2,1)}, bf16[512,4096]{1,0:T(8,128)(2,1)}, bf16[512,4096]{1,0:T(8,128)(2,1)}) custom-call(s32[1]{0:T(128)} %bitcast.mine, bf16[512,512]{1,0:T(8,128)(2,1)} %bitcast.291, bf16[512,1024]{1,0:T(8,128)(2,1)} %bitcast.284, bf16[512,1024]{1,0:T(8,128)(2,1)} %output_weight.3, ...), custom_call_target="tpu_custom_call" | custom-call | flops 8589934592 | bytes 25165824 | tf_op jit(solution)/shard_map/pallas_call | solution.py:194
  53.4 14.1 %shard_map.257 = (f32[512,1024]{1,0:T(8,128)}, bf16[512,512]{1,0:T(8,128)(2,1)}, bf16[256,1024]{1,0:T(8,128)(2,1)}, bf16[256,1024]{1,0:T(8,128)(2,1)}, f32[8,1024]{1,0:T(8,128)}) custom-call(s32[1]{0:T(128)} %bitcast.mine, bf16[512,4096]{1,0:T(8,128)(2,1)} %get-tuple-element.53.inner_grad, bf16[1024,4096]{1,0:T(8,128)(2,1)} %inner_weight.3, ...), custom_call_target="tpu_custom_call" | custom-call | flops 5368709120 | bytes 16777216 | tf_op jit(solution)/shard_map/pallas_call | solution.py:318
  67.5 37.7 %shard_map.258 = (bf16[8,640,1024]{2,1,0:T(8,128)(2,1)}, bf16[8,64,512]{2,1,0:T(8,128)(2,1)}, bf16[512,1024]{1,0:T(8,128)(2,1)}, bf16[512,1024]{1,0:T(8,128)(2,1...) custom-call(s32[8]{0:T(128)} %dynamic_slice.3.lengths, ...), custom_call_target="tpu_custom_call" | custom-call | flops 16106127360 | bytes 31457280 | tf_op jit(solution)/shard_map/pallas_call | solution.py:480
  106.3 5.6 %shard_map.261 = (bf16[512,2048]{1,0:T(8,128)(2,1)}, bf16[512,2048]{1,0:T(8,128)(2,1)}) custom-call(bf16[512,512]{1,0:T(8,128)(2,1)} %get-tuple-element.68.hidden_keep, bf16[512,512]{1,0:T(8,128)(2,1)} %get-tuple-element.69.hidden_send, bf16[512,4096]{1,0:T(8,128)(2,1)} %get-tuple-element.53.inner_grad), custom_call_target="tpu_custom_call" | custom-call | flops 2147483648 | bytes 6291456 | tf_op jit(solution)/shard_map/pallas_call | solution.py:263
  112.4 5.7 %shard_map.260 = (bf16[512,2048]{1,0:T(8,128)(2,1)}, bf16[512,2048]{1,0:T(8,128)(2,1)}) custom-call(bf16[512,512]{1,0:T(8,128)(2,1)} %get-tuple-element.68.hidden_keep, bf16[512,512]{1,0:T(8,128)(2,1)} %get-tuple-element.69.hidden_send, bf16[512,4096]{1,0:T(8,128)(2,1)} %get-tuple-element.53.inner_grad), custom_call_target="tpu_custom_call" | custom-call | flops 2147483648 | bytes 6291456 | tf_op jit(solution)/shard_map/pallas_call | solution.py:263
  118.1 22.1 %shard_map.256 = bf16[512,1024]{1,0:T(8,128)(2,1)} custom-call(bf16[512,4096]{1,0:T(8,128)(2,1)} %get-tuple-element.48.activation, bf16[4096,1024]{1,0:T(8,128)(2,1)} %outer_weight.3, f32[512,1024]{1,0:T(8,128)} %get-tuple-element.49.residual), custom_call_target="tpu_custom_call" | custom-call | flops 4294967296 | bytes 15728640 | tf_op jit(solution)/shard_map/pallas_call | solution.py:365
  140.2 6.4 %shard_map.263 = (bf16[2048,512]{1,0:T(8,128)(2,1)}, bf16[2048,512]{1,0:T(8,128)(2,1)}) custom-call(s32[1]{0:T(128)} %bitcast.mine, bf16[512,4096]{1,0:T(8,128)(2,1)} %get-tuple-element.48.activation, bf16[512,1024]{1,0:T(8,128)(2,1)} %bitcast.282), custom_call_target="tpu_custom_call" | custom-call | flops 2147483648 | bytes 8388608 | tf_op jit(solution)/shard_map/pallas_call | solution.py:234
  146.6 6.6 %shard_map.262 = (bf16[2048,512]{1,0:T(8,128)(2,1)}, bf16[2048,512]{1,0:T(8,128)(2,1)}) custom-call(s32[1]{0:T(128)} %bitcast.mine, bf16[512,4096]{1,0:T(8,128)(2,1)} %get-tuple-element.48.activation, bf16[512,1024]{1,0:T(8,128)(2,1)} %bitcast.283), custom_call_target="tpu_custom_call" | custom-call | flops 2147483648 | bytes 8388608 | tf_op jit(solution)/shard_map/pallas_call | solution.py:234
  160.4 29.1 %shard_map.259 = (bf16[8,576,1024]{2,1,0:T(8,128)(2,1)}, bf16[8,64,1024]{2,1,0:T(8,128)(2,1)}) custom-call(bf16[8,576,1024]{2,1,0:T(8,128)(2,1)} %media.3, bf16[8,64,1024]{2,1,0:T(8,128)(2,1)} %latents.3, bf16[8,640,1024]{2,1,0:T(8,128)(2,1)} %get-tuple-element.57.keyval_grad, bf16[8,64,512]{2,1,0:T(8,128)(2,1)} %get-tuple-element.58.query_grad, ...), custom_call_target="tpu_custom_call" | custom-call | flops 12884901888 | bytes 31457280 | tf_op jit(solution)/shard_map/pallas_call | solution.py:537
  200.1 11.3 %collective-permute-done.36 = f32[2,2,2,32,128]{3,4,1,0,2:T(8,128)S(1)} collective-permute-done((f32[2,2,2,32,128]{3,4,1,0,2:T(8,128)S(1)}, f32[2,2,2,32,128]{3,4,1,0,2:T(8,128)S(1)}, u32[]{:S(2)}, u32[]{:S(2)}) %collective-permute-start.36) | collective-permute-done | bytes 131104 | tf_op jit(solution)/shard_map/ppermute | solution.py:555
  213.3 6.2 %collective-permute-done.37 = f32[2,2,32,128]{2,3,1,0:T(8,128)S(1)} collective-permute-done((f32[2,2,32,128]{2,3,1,0:T(8,128)S(1)}, f32[2,2,32,128]{2,3,1,0:T(8,128)S(1)}, u32[]{:S(2)}, u32[]{:S(2)}) %collective-permute-start.37) | collective-permute-done | bytes 65568 | tf_op jit(solution)/shard_map/ppermute | solution.py:555
  221.4 3.3 collective-permute-done.38
  224.7 2.7 collective-permute-start.39
  235.1 5.7 %collective-permute-done.1 = bf16[2,2,2,32,512]{4,3,1,0,2:T(8,128)(2,1)S(1)} collective-permute-done((bf16[2,2,2,32,512]{4,3,1,0,2:T(8,128)(2,1)S(1)}, bf16[2,2,2,32,512]{4,3,1,0,2:T(8,128)(2,1)S(1)}, u32[]{:S(2)}, u32[]{:S(2)}) %collective-permute-start.1) | collective-permute-done | bytes 262176 | tf_op jit(solution)/shard_map/ppermute | solution.py:555
  240.8 5.2 %collective-permute-done.11 = bf16[2,2,2,16,1024]{4,3,1,0,2:T(8,128)(2,1)S(1)} collective-permute-done((bf16[2,2,2,16,1024]{4,3,1,0,2:T(8,128)(2,1)S(1)}, bf16[2,2,2,16,1024]{4,3,1,0,2:T(8,128)(2,1)S(1)}, u32[]{:S(2)}, u32[]{:S(2)}) %collective-permute-start.11) | collective-permute-done | bytes 262176 | tf_op jit(solution)/shard_map/ppermute | solution.py:555
  249.7 2.7 collective-permute-done.2
  257.1 8.1 %collective-permute-done.6 = bf16[2,2,2,32,1024]{4,3,1,0,2:T(8,128)(2,1)S(1)} collective-permute-done((bf16[2,2,2,32,1024]{4,3,1,0,2:T(8,128)(2,1)S(1)}, bf16[2,2,2,32,1024]{4,3,1,0,2:T(8,128)(2,1)S(1)}, u32[]{:S(2)}, u32[]{:S(2)}) %collective-permute-start.6) | collective-permute-done | bytes 524320 | tf_op jit(solution)/shard_map/ppermute | solution.py:555
  269.5 4.0 %collective-permute-done.7 = bf16[2,2,32,1024]{3,2,1,0:T(8,128)(2,1)S(1)} collective-permute-done((bf16[2,2,32,1024]{3,2,1,0:T(8,128)(2,1)S(1)}, bf16[2,2,32,1024]{3,2,1,0:T(8,128)(2,1)S(1)}, u32[]{:S(2)}, u32[]{:S(2)}) %collective-permute-start.7) | collective-permute-done | bytes 262176 | tf_op jit(solution)/shard_map/ppermute | solution.py:555
  273.5 3.1 collective-permute-start.4
  279.3 4.3 %collective-permute-done.8 = bf16[2,32,1024]{2,1,0:T(8,128)(2,1)S(1)} collective-permute-done((bf16[2,32,1024]{2,1,0:T(8,128)(2,1)S(1)}, bf16[2,32,1024]{2,1,0:T(8,128)(2,1)S(1)}, u32[]{:S(2)}, u32[]{:S(2)}) %collective-permute-start.8) | collective-permute-done | bytes 131104 | tf_op jit(solution)/shard_map/ppermute | solution.py:555
  283.6 2.8 collective-permute-start.14
  288.5 2.7 collective-permute-start.9
  308.3 14.8 %collective-permute-done.21 = bf16[2,2,2,32,2048]{4,3,1,0,2:T(8,128)(2,1)S(1)} collective-permute-done((bf16[2,2,2,32,2048]{4,3,1,0,2:T(8,128)(2,1)S(1)}, bf16[2,2,2,32,2048]{4,3,1,0,2:T(8,128)(2,1)S(1)}, u32[]{:S(2)}, u32[]{:S(2)}) %collective-permute-start.21) | collective-permute-done | bytes 1048608 | tf_op jit(solution)/shard_map/ppermute | solution.py:555
  327.3 18.3 %collective-permute-done.31 = bf16[2,2,2,128,512]{4,3,1,0,2:T(8,128)(2,1)S(1)} collective-permute-done((bf16[2,2,2,128,512]{4,3,1,0,2:T(8,128)(2,1)S(1)}, bf16[2,2,2,128,512]{4,3,1,0,2:T(8,128)(2,1)S(1)}, u32[]{:S(2)}, u32[]{:S(2)}) %collective-permute-start.31) | collective-permute-done | bytes 1048608 | tf_op jit(solution)/shard_map/ppermute | solution.py:555
  349.7 6.9 %collective-permute-done.22 = bf16[2,2,32,2048]{3,2,1,0:T(8,128)(2,1)S(1)} collective-permute-done((bf16[2,2,32,2048]{3,2,1,0:T(8,128)(2,1)S(1)}, bf16[2,2,32,2048]{3,2,1,0:T(8,128)(2,1)S(1)}, u32[]{:S(2)}, u32[]{:S(2)}) %collective-permute-start.22) | collective-permute-done | bytes 524320 | tf_op jit(solution)/shard_map/ppermute | solution.py:555
  359.0 3.2 collective-permute-done.32
  364.6 5.6 %collective-permute-done.23 = bf16[2,32,2048]{2,1,0:T(8,128)(2,1)S(1)} collective-permute-done((bf16[2,32,2048]{2,1,0:T(8,128)(2,1)S(1)}, bf16[2,32,2048]{2,1,0:T(8,128)(2,1)S(1)}, u32[]{:S(2)}, u32[]{:S(2)}) %collective-permute-start.23) | collective-permute-done | bytes 262176 | tf_op jit(solution)/shard_map/ppermute | solution.py:555
  373.2 2.7 collective-permute-start.19
  377.6 5.1 %collective-permute-start.34 = (bf16[128,512]{1,0:T(8,128)(2,1)S(1)}, bf16[128,512]{1,0:T(8,128)(2,1)S(1)}, u32[]{:S(2)}, u32[]{:S(2)}) collective-permute-start(bf16[128,512]{1,0:T(8,128)(2,1)S(1)} %fusion.50), channel_id=1, source_target_pairs={{0,16},{1,17},{2,18},{3,19},{4,20},{5,21},{6,22},{7,23},{8,24},{9,... | collective-permute-start | bytes 393224 | tf_op jit(solution)/shard_map/ppermute | solution.py:555
  383.0 2.7 collective-permute-start.29
  388.6 2.8 collective-permute-done.29
  (166 shorter events, 90.0 us)
Async XLA Ops:
  105.2 85.9 %collective-permute-start.35 = (f32[512,128]{1,0:T(8,128)}, f32[512,128]{1,0:T(8,128)S(1)}, u32[]{:S(2)}, u32[]{:S(2)}) collective-permute-start(f32[512,128]{1,0:T(8,128)} %get-tuple-element.79), channel_id=1, source_target_pairs={{0,1},{1,0},{2,3},{3,2},{4,5},{5,4},{6,7},{7,6},{8,9},{9,8},{10,11... | collective-permute-start | bytes 786440 | tf_op jit(solution)/shard_map/ppermute | solution.py:555
  105.7 124.7 %collective-permute-start = (bf16[512,512]{1,0:T(8,128)(2,1)}, bf16[512,512]{1,0:T(8,128)(2,1)}, u32[]{:S(2)}, u32[]{:S(2)}) collective-permute-start(bf16[512,512]{1,0:T(8,128)(2,1)} %get-tuple-element.63), channel_id=1, source_target_pairs={{0,1},{1,0},{2,3},{3,2},{4,5},{5,4},{6,7},{7,6},{8,9},{9,8},{10,11... | collective-permute-start | bytes 1572872 | tf_op jit(solution)/shard_map/ppermute | solution.py:555
  105.8 127.4 %collective-permute-start.10 = (bf16[256,1024]{1,0:T(8,128)(2,1)}, bf16[256,1024]{1,0:T(8,128)(2,1)}, u32[]{:S(2)}, u32[]{:S(2)}) collective-permute-start(bf16[256,1024]{1,0:T(8,128)(2,1)} %get-tuple-element.67), channel_id=1, source_target_pairs={{0,1},{1,0},{2,3},{3,2},{4,5},{5,4},{6,7},{7,6},{8,9},{9,8},{10,11... | collective-permute-start | bytes 1572872 | tf_op jit(solution)/shard_map/ppermute | solution.py:555
  106.3 141.4 %collective-permute-start.5 = (bf16[512,1024]{1,0:T(8,128)(2,1)}, bf16[512,1024]{1,0:T(8,128)(2,1)}, u32[]{:S(2)}, u32[]{:S(2)}) collective-permute-start(bf16[512,1024]{1,0:T(8,128)(2,1)} %get-tuple-element.65), channel_id=1, source_target_pairs={{0,1},{1,0},{2,3},{3,2},{4,5},{5,4},{6,7},{7,6},{8,9},{9,8},{10,11... | collective-permute-start | bytes 3145736 | tf_op jit(solution)/shard_map/ppermute | solution.py:555
  112.0 182.7 %collective-permute-start.20 = (bf16[512,2048]{1,0:T(8,128)(2,1)}, bf16[512,2048]{1,0:T(8,128)(2,1)}, u32[]{:S(2)}, u32[]{:S(2)}) collective-permute-start(bf16[512,2048]{1,0:T(8,128)(2,1)} %get-tuple-element.73), channel_id=1, source_target_pairs={{0,1},{1,0},{2,3},{3,2},{4,5},{5,4},{6,7},{7,6},{8,9},{9,8},{10,11... | collective-permute-start | bytes 6291464 | tf_op jit(solution)/shard_map/ppermute | solution.py:555
  196.2 15.2 %collective-permute-start.36 = (f32[2,2,2,32,128]{3,4,1,0,2:T(8,128)S(1)}, f32[2,2,2,32,128]{3,4,1,0,2:T(8,128)S(1)}, u32[]{:S(2)}, u32[]{:S(2)}) collective-permute-start(f32[2,2,2,32,128]{3,4,1,0,2:T(8,128)S(1)} %add_bitcast_fusion), channel_id=1, source_target_pairs={{0,2},{1,3},{2,0},{3,1},{4,6},{5,7},{6,4},{7,5},{8,10},{9,11},{10,... | collective-permute-start | bytes 393224 | tf_op jit(solution)/shard_map/ppermute | solution.py:555
  211.4 8.1 %collective-permute-start.37 = (f32[2,2,32,128]{2,3,1,0:T(8,128)S(1)}, f32[2,2,32,128]{2,3,1,0:T(8,128)S(1)}, u32[]{:S(2)}, u32[]{:S(2)}) collective-permute-start(f32[2,2,32,128]{2,3,1,0:T(8,128)S(1)} %get-tuple-element.105), channel_id=1, source_target_pairs={{0,4},{1,5},{2,6},{3,7},{4,0},{5,1},{6,2},{7,3},{8,12},{9,13},{10,... | collective-permute-start | bytes 196616 | tf_op jit(solution)/shard_map/ppermute | solution.py:555
  229.9 68.7 %collective-permute-start.15 = (bf16[512,2048]{1,0:T(8,128)(2,1)S(1)}, bf16[512,2048]{1,0:T(8,128)(2,1)S(1)}, u32[]{:S(2)}, u32[]{:S(2)}) collective-permute-start(bf16[512,2048]{1,0:T(8,128)(2,1)S(1)} %copy-done.16), channel_id=1, source_target_pairs={{0,1},{1,0},{2,3},{3,2},{4,5},{5,4},{6,7},{7,6},{8,9},{9,8},{10,11... | collective-permute-start | bytes 6291464 | tf_op jit(solution)/shard_map/ppermute | solution.py:555
  231.6 9.2 %collective-permute-start.1 = (bf16[2,2,2,32,512]{4,3,1,0,2:T(8,128)(2,1)S(1)}, bf16[2,2,2,32,512]{4,3,1,0,2:T(8,128)(2,1)S(1)}, u32[]{:S(2)}, u32[]{:S(2)}) collective-permute-start(bf16[2,2,2,32,512]{4,3,1,0,2:T(8,128)(2,1)S(1)} %fusion.19), channel_id=1, source_target_pairs={{0,2},{1,3},{2,0},{3,1},{4,6},{5,7},{6,4},{7,5},{8,10},{9,11},{10,... | collective-permute-start | bytes 786440 | tf_op jit(solution)/shard_map/ppermute | solution.py:555
  234.4 11.6 %collective-permute-start.11 = (bf16[2,2,2,16,1024]{4,3,1,0,2:T(8,128)(2,1)S(1)}, bf16[2,2,2,16,1024]{4,3,1,0,2:T(8,128)(2,1)S(1)}, u32[]{:S(2)}, u32[]{:S(2)}) collective-permute-start(bf16[2,2,2,16,1024]{4,3,1,0,2:T(8,128)(2,1)S(1)} %fusion.23), channel_id=1, source_target_pairs={{0,2},{1,3},{2,0},{3,1},{4,6},{5,7},{6,4},{7,5},{8,10},{9,11},{10,... | collective-permute-start | bytes 786440 | tf_op jit(solution)/shard_map/ppermute | solution.py:555
  240.8 61.2 %collective-permute-start.30 = (bf16[2048,512]{1,0:T(8,128)(2,1)S(1)}, bf16[2048,512]{1,0:T(8,128)(2,1)S(1)}, u32[]{:S(2)}, u32[]{:S(2)}) collective-permute-start(bf16[2048,512]{1,0:T(8,128)(2,1)S(1)} %copy-done.15), channel_id=1, source_target_pairs={{0,1},{1,0},{2,3},{3,2},{4,5},{5,4},{6,7},{7,6},{8,9},{9,8},{10,11... | collective-permute-start | bytes 6291464 | tf_op jit(solution)/shard_map/ppermute | solution.py:555
  247.6 7.6 %collective-permute-start.12 = (bf16[2,2,16,1024]{3,2,1,0:T(8,128)(2,1)S(1)}, bf16[2,2,16,1024]{3,2,1,0:T(8,128)(2,1)S(1)}, u32[]{:S(2)}, u32[]{:S(2)}) collective-permute-start(bf16[2,2,16,1024]{3,2,1,0:T(8,128)(2,1)S(1)} %get-tuple-element.123), channel_id=1, source_target_pairs={{0,4},{1,5},{2,6},{3,7},{4,0},{5,1},{6,2},{7,3},{8,12},{9,13},{10,... | collective-permute-start | bytes 393224 | tf_op jit(solution)/shard_map/ppermute | solution.py:555
  252.4 12.8 %collective-permute-start.6 = (bf16[2,2,2,32,1024]{4,3,1,0,2:T(8,128)(2,1)S(1)}, bf16[2,2,2,32,1024]{4,3,1,0,2:T(8,128)(2,1)S(1)}, u32[]{:S(2)}, u32[]{:S(2)}) collective-permute-start(bf16[2,2,2,32,1024]{4,3,1,0,2:T(8,128)(2,1)S(1)} %fusion.9), channel_id=1, source_target_pairs={{0,4},{1,5},{2,6},{3,7},{4,0},{5,1},{6,2},{7,3},{8,12},{9,13},{10,... | collective-permute-start | bytes 1572872 | tf_op jit(solution)/shard_map/ppermute | solution.py:555
  255.2 11.8 %collective-permute-start.3 = (bf16[2,32,512]{2,1,0:T(8,128)(2,1)S(1)}, bf16[2,32,512]{2,1,0:T(8,128)(2,1)S(1)}, u32[]{:S(2)}, u32[]{:S(2)}) collective-permute-start(bf16[2,32,512]{2,1,0:T(8,128)(2,1)S(1)} %get-tuple-element.143), channel_id=1, source_target_pairs={{0,8},{1,9},{2,10},{3,11},{4,12},{5,13},{6,14},{7,15},{8,0},{9,1},... | collective-permute-start | bytes 196616 | tf_op jit(solution)/shard_map/ppermute | solution.py:555
  267.1 6.4 %collective-permute-start.7 = (bf16[2,2,32,1024]{3,2,1,0:T(8,128)(2,1)S(1)}, bf16[2,2,32,1024]{3,2,1,0:T(8,128)(2,1)S(1)}, u32[]{:S(2)}, u32[]{:S(2)}) collective-permute-start(bf16[2,2,32,1024]{3,2,1,0:T(8,128)(2,1)S(1)} %get-tuple-element.115), channel_id=1, source_target_pairs={{0,2},{1,3},{2,0},{3,1},{4,6},{5,7},{6,4},{7,5},{8,10},{9,11},{10,... | collective-permute-start | bytes 786440 | tf_op jit(solution)/shard_map/ppermute | solution.py:555
  269.4 34.5 %collective-permute-start.25 = (bf16[2048,512]{1,0:T(8,128)(2,1)S(1)}, bf16[2048,512]{1,0:T(8,128)(2,1)S(1)}, u32[]{:S(2)}, u32[]{:S(2)}) collective-permute-start(bf16[2048,512]{1,0:T(8,128)(2,1)S(1)} %copy-done.14), channel_id=1, source_target_pairs={{0,1},{1,0},{2,3},{3,2},{4,5},{5,4},{6,7},{7,6},{8,9},{9,8},{10,11... | collective-permute-start | bytes 6291464 | tf_op jit(solution)/shard_map/ppermute | solution.py:555
  297.0 26.2 %collective-permute-start.21 = (bf16[2,2,2,32,2048]{4,3,1,0,2:T(8,128)(2,1)S(1)}, bf16[2,2,2,32,2048]{4,3,1,0,2:T(8,128)(2,1)S(1)}, u32[]{:S(2)}, u32[]{:S(2)}) collective-permute-start(bf16[2,2,2,32,2048]{4,3,1,0,2:T(8,128)(2,1)S(1)} %fusion.3), channel_id=1, source_target_pairs={{0,2},{1,3},{2,0},{3,1},{4,6},{5,7},{6,4},{7,5},{8,10},{9,11},{10,... | collective-permute-start | bytes 3145736 | tf_op jit(solution)/shard_map/ppermute | solution.py:555
  300.2 26.2 %collective-permute-start.16 = (bf16[2,2,2,32,2048]{4,3,1,0,2:T(8,128)(2,1)S(1)}, bf16[2,2,2,32,2048]{4,3,1,0,2:T(8,128)(2,1)S(1)}, u32[]{:S(2)}, u32[]{:S(2)}) collective-permute-start(bf16[2,2,2,32,2048]{4,3,1,0,2:T(8,128)(2,1)S(1)} %fusion.1), channel_id=1, source_target_pairs={{0,4},{1,5},{2,6},{3,7},{4,0},{5,1},{6,2},{7,3},{8,12},{9,13},{10,... | collective-permute-start | bytes 3145736 | tf_op jit(solution)/shard_map/ppermute | solution.py:555
  303.5 42.1 %collective-permute-start.31 = (bf16[2,2,2,128,512]{4,3,1,0,2:T(8,128)(2,1)S(1)}, bf16[2,2,2,128,512]{4,3,1,0,2:T(8,128)(2,1)S(1)}, u32[]{:S(2)}, u32[]{:S(2)}) collective-permute-start(bf16[2,2,2,128,512]{4,3,1,0,2:T(8,128)(2,1)S(1)} %fusion.7), channel_id=1, source_target_pairs={{0,2},{1,3},{2,0},{3,1},{4,6},{5,7},{6,4},{7,5},{8,10},{9,11},{10,... | collective-permute-start | bytes 3145736 | tf_op jit(solution)/shard_map/ppermute | solution.py:555
  305.5 43.4 %collective-permute-start.26 = (bf16[2,2,2,128,512]{4,3,1,0,2:T(8,128)(2,1)S(1)}, bf16[2,2,2,128,512]{4,3,1,0,2:T(8,128)(2,1)S(1)}, u32[]{:S(2)}, u32[]{:S(2)}) collective-permute-start(bf16[2,2,2,128,512]{4,3,1,0,2:T(8,128)(2,1)S(1)} %fusion.5), channel_id=1, source_target_pairs={{0,4},{1,5},{2,6},{3,7},{4,0},{5,1},{6,2},{7,3},{8,12},{9,13},{10,... | collective-permute-start | bytes 3145736 | tf_op jit(solution)/shard_map/ppermute | solution.py:555
  323.5 33.1 %collective-permute-start.22 = (bf16[2,2,32,2048]{3,2,1,0:T(8,128)(2,1)S(1)}, bf16[2,2,32,2048]{3,2,1,0:T(8,128)(2,1)S(1)}, u32[]{:S(2)}, u32[]{:S(2)}) collective-permute-start(bf16[2,2,32,2048]{3,2,1,0:T(8,128)(2,1)S(1)} %get-tuple-element.99), channel_id=1, source_target_pairs={{0,4},{1,5},{2,6},{3,7},{4,0},{5,1},{6,2},{7,3},{8,12},{9,13},{10,... | collective-permute-start | bytes 1572872 | tf_op jit(solution)/shard_map/ppermute | solution.py:555
  326.8 31.7 %collective-permute-start.17 = (bf16[2,2,32,2048]{3,2,1,0:T(8,128)(2,1)S(1)}, bf16[2,2,32,2048]{3,2,1,0:T(8,128)(2,1)S(1)}, u32[]{:S(2)}, u32[]{:S(2)}) collective-permute-start(bf16[2,2,32,2048]{3,2,1,0:T(8,128)(2,1)S(1)} %get-tuple-element.93), channel_id=1, source_target_pairs={{0,2},{1,3},{2,0},{3,1},{4,6},{5,7},{6,4},{7,5},{8,10},{9,11},{10,... | collective-permute-start | bytes 1572872 | tf_op jit(solution)/shard_map/ppermute | solution.py:555
  345.9 16.3 %collective-permute-start.32 = (bf16[2,2,128,512]{3,2,1,0:T(8,128)(2,1)S(1)}, bf16[2,2,128,512]{3,2,1,0:T(8,128)(2,1)S(1)}, u32[]{:S(2)}, u32[]{:S(2)}) collective-permute-start(bf16[2,2,128,512]{3,2,1,0:T(8,128)(2,1)S(1)} %get-tuple-element.87), channel_id=1, source_target_pairs={{0,4},{1,5},{2,6},{3,7},{4,0},{5,1},{6,2},{7,3},{8,12},{9,13},{10,... | collective-permute-start | bytes 1572872 | tf_op jit(solution)/shard_map/ppermute | solution.py:555
  349.2 14.9 %collective-permute-start.27 = (bf16[2,2,128,512]{3,2,1,0:T(8,128)(2,1)S(1)}, bf16[2,2,128,512]{3,2,1,0:T(8,128)(2,1)S(1)}, u32[]{:S(2)}, u32[]{:S(2)}) collective-permute-start(bf16[2,2,128,512]{3,2,1,0:T(8,128)(2,1)S(1)} %get-tuple-element.81), channel_id=1, source_target_pairs={{0,2},{1,3},{2,0},{3,1},{4,6},{5,7},{6,4},{7,5},{8,10},{9,11},{10,... | collective-permute-start | bytes 1572872 | tf_op jit(solution)/shard_map/ppermute | solution.py:555
  356.7 13.5 %collective-permute-start.23 = (bf16[2,32,2048]{2,1,0:T(8,128)(2,1)S(1)}, bf16[2,32,2048]{2,1,0:T(8,128)(2,1)S(1)}, u32[]{:S(2)}, u32[]{:S(2)}) collective-permute-start(bf16[2,32,2048]{2,1,0:T(8,128)(2,1)S(1)} %get-tuple-element.113), channel_id=1, source_target_pairs={{0,8},{1,9},{2,10},{3,11},{4,12},{5,13},{6,14},{7,15},{8,0},{9,1},... | collective-permute-start | bytes 786440 | tf_op jit(solution)/shard_map/ppermute | solution.py:555
  358.6 14.5 %collective-permute-start.18 = (bf16[2,32,2048]{2,1,0:T(8,128)(2,1)S(1)}, bf16[2,32,2048]{2,1,0:T(8,128)(2,1)S(1)}, u32[]{:S(2)}, u32[]{:S(2)}) collective-permute-start(bf16[2,32,2048]{2,1,0:T(8,128)(2,1)S(1)} %get-tuple-element.111), channel_id=1, source_target_pairs={{0,8},{1,9},{2,10},{3,11},{4,12},{5,13},{6,14},{7,15},{8,0},{9,1},... | collective-permute-start | bytes 786440 | tf_op jit(solution)/shard_map/ppermute | solution.py:555
  362.3 15.2 %collective-permute-start.33 = (bf16[2,128,512]{2,1,0:T(8,128)(2,1)S(1)}, bf16[2,128,512]{2,1,0:T(8,128)(2,1)S(1)}, u32[]{:S(2)}, u32[]{:S(2)}) collective-permute-start(bf16[2,128,512]{2,1,0:T(8,128)(2,1)S(1)} %get-tuple-element.109), channel_id=1, source_target_pairs={{0,8},{1,9},{2,10},{3,11},{4,12},{5,13},{6,14},{7,15},{8,0},{9,1},... | collective-permute-start | bytes 786440 | tf_op jit(solution)/shard_map/ppermute | solution.py:555
  364.2 18.7 %collective-permute-start.28 = (bf16[2,128,512]{2,1,0:T(8,128)(2,1)S(1)}, bf16[2,128,512]{2,1,0:T(8,128)(2,1)S(1)}, u32[]{:S(2)}, u32[]{:S(2)}) collective-permute-start(bf16[2,128,512]{2,1,0:T(8,128)(2,1)S(1)} %get-tuple-element.107), channel_id=1, source_target_pairs={{0,8},{1,9},{2,10},{3,11},{4,12},{5,13},{6,14},{7,15},{8,0},{9,1},... | collective-permute-start | bytes 786440 | tf_op jit(solution)/shard_map/ppermute | solution.py:555
  370.2 15.5 %collective-permute-start.24 = (bf16[32,2048]{1,0:T(8,128)(2,1)S(1)}, bf16[32,2048]{1,0:T(8,128)(2,1)S(1)}, u32[]{:S(2)}, u32[]{:S(2)}) collective-permute-start(bf16[32,2048]{1,0:T(8,128)(2,1)S(1)} %fusion.46), channel_id=1, source_target_pairs={{0,16},{1,17},{2,18},{3,19},{4,20},{5,21},{6,22},{7,23},{8,24},{9,... | collective-permute-start | bytes 393224 | tf_op jit(solution)/shard_map/ppermute | solution.py:555
  373.2 12.6 %collective-permute-start.19 = (bf16[32,2048]{1,0:T(8,128)(2,1)S(1)}, bf16[32,2048]{1,0:T(8,128)(2,1)S(1)}, u32[]{:S(2)}, u32[]{:S(2)}) collective-permute-start(bf16[32,2048]{1,0:T(8,128)(2,1)S(1)} %fusion.44), channel_id=1, source_target_pairs={{0,16},{1,17},{2,18},{3,19},{4,20},{5,21},{6,22},{7,23},{8,24},{9,... | collective-permute-start | bytes 393224 | tf_op jit(solution)/shard_map/ppermute | solution.py:555
  377.6 11.0 %collective-permute-start.34 = (bf16[128,512]{1,0:T(8,128)(2,1)S(1)}, bf16[128,512]{1,0:T(8,128)(2,1)S(1)}, u32[]{:S(2)}, u32[]{:S(2)}) collective-permute-start(bf16[128,512]{1,0:T(8,128)(2,1)S(1)} %fusion.50), channel_id=1, source_target_pairs={{0,16},{1,17},{2,18},{3,19},{4,20},{5,21},{6,22},{7,23},{8,24},{9,... | collective-permute-start | bytes 393224 | tf_op jit(solution)/shard_map/ppermute | solution.py:555
  383.0 8.4 %collective-permute-start.29 = (bf16[128,512]{1,0:T(8,128)(2,1)S(1)}, bf16[128,512]{1,0:T(8,128)(2,1)S(1)}, u32[]{:S(2)}, u32[]{:S(2)}) collective-permute-start(bf16[128,512]{1,0:T(8,128)(2,1)S(1)} %fusion.48), channel_id=1, source_target_pairs={{0,16},{1,17},{2,18},{3,19},{4,20},{5,21},{6,22},{7,23},{8,24},{9,... | collective-permute-start | bytes 393224 | tf_op jit(solution)/shard_map/ppermute | solution.py:555
  (25 other events, 198.5 us)

commit v2 on v1

v2 whole, which is shorter than its diff:
```python
import functools

import jax
import jax.numpy as jnp
from jax import lax
from jax.experimental import pallas as pl
from jax.experimental.pallas import tpu as pltpu
from jax.sharding import PartitionSpec as P

HEAD_DIM = 64
GROUP = 256
norm_eps = 1e-05
masked_score = -1e30
bf16, f32 = jnp.bfloat16, jnp.float32
VMEM_LIMIT = 56 << 20


def shape(dims, dtype):
    return jax.ShapeDtypeStruct(dims, dtype)


def dot(left, right, left_dim=1, right_dim=0):
    return lax.dot_general(
        left, right, (((left_dim,), (right_dim,)), ((), ())), preferred_element_type=f32
    )


def call(body, flops, bytes_accessed, **kwargs):
    return pl.pallas_call(
        body,
        compiler_params=pltpu.CompilerParams(vmem_limit_bytes=VMEM_LIMIT),
        cost_estimate=pl.CostEstimate(
            flops=flops, bytes_accessed=bytes_accessed, transcendentals=0
        ),
        **kwargs,
    )


def unread(arrays):
    return [pl.BlockSpec(memory_space=pl.ANY)] * len(arrays)


def normalise(values):
    centre = values - jnp.mean(values, axis=-1, keepdims=True)
    spread = jnp.mean(centre * centre, axis=-1, keepdims=True)
    factor = lax.rsqrt(spread + norm_eps)
    return centre * factor, factor


def norm_back(grad, normed, factor, gain):
    scaled = grad * gain
    average = jnp.mean(scaled, axis=-1, keepdims=True)
    along = jnp.mean(scaled * normed, axis=-1, keepdims=True)
    return factor * (scaled - average - normed * along)


def own_head():
    row = lax.broadcasted_iota(jnp.int32, (GROUP, GROUP), 0) // HEAD_DIM
    column = lax.broadcasted_iota(jnp.int32, (GROUP, GROUP), 1) // HEAD_DIM
    return row == column


def stack_heads(rows, own):
    repeated = jnp.concatenate([rows.astype(f32)] * (GROUP // HEAD_DIM), axis=0)
    return jnp.where(own, repeated, 0.0).astype(bf16)


def unstack_heads(full, own):
    full = jnp.where(own, full, 0.0)
    rows = full.shape[0] // (GROUP // HEAD_DIM)
    return sum(full[h * rows : (h + 1) * rows] for h in range(GROUP // HEAD_DIM))


def score_columns(key_group, stacked, length, media_rows):
    scores = dot(key_group, stacked, 1, 1)
    position = lax.broadcasted_iota(jnp.int32, scores.shape, 0)
    usable = (position < length) | (position >= media_rows)
    return jnp.where(usable, scores, masked_score)


def attend_body(
    lengths, mine, media, latents, query_weight, keyval_weight, media_gain, media_bias,
    latent_gain, latent_bias, media_low, latent_low, keyval, query, mixed, log_total, latent_keyval,
):
    step = pl.program_id(0)
    media_rows = media.shape[1]
    latent_rows = keyval.shape[1] - media_rows
    inner = query_weight.shape[1]

    @pl.when(step == 0)
    def _():
        normed, _ = normalise(latents[...].astype(f32))
        latent_low[...] = (normed * latent_gain[...] + latent_bias[...]).astype(bf16)
        query[...] = (dot(latent_low[...], query_weight[...]) * 0.125).astype(bf16)
        latent_keyval[...] = dot(latent_low[...], keyval_weight[...]).astype(bf16)

    normed, _ = normalise(media[0].astype(f32))
    media_low[...] = (normed * media_gain[...] + media_bias[...]).astype(bf16)
    keyval[0, :media_rows] = dot(media_low[...], keyval_weight[...]).astype(bf16)
    here = pl.ds(pl.multiple_of(step * latent_rows, latent_rows), latent_rows)
    keyval[0, media_rows:] = latent_keyval[here, :]
    own = own_head()
    for g in range(inner // GROUP):
        at = pl.ds(g * GROUP, GROUP)
        stacked = stack_heads(query[here, at], own)
        scores = score_columns(keyval[0, :, at], stacked, lengths[mine[1] + step], media_rows)
        top = jnp.max(scores, axis=0, keepdims=True)
        exps = jnp.exp(scores - top)
        total = jnp.sum(exps, axis=0, keepdims=True)
        log_total[0, :, at] = top + jnp.log(total)
        prob_low = (exps * (1.0 / total)).astype(bf16)
        full = dot(prob_low, keyval[0, :, pl.ds(inner + g * GROUP, GROUP)], 0, 0)
        mixed[:, at] = unstack_heads(full, own).astype(bf16)


def attend(lengths, mine, media, latents, query_weight, keyval_weight, gains):
    images, media_rows, width = media.shape
    rows = latents.shape[0]
    latent_rows = rows // images
    inner = query_weight.shape[1]
    keys = media_rows + latent_rows

    def image(count, columns):
        return pl.BlockSpec((1, count, columns), lambda i, *_: (i, 0, 0))

    def whole(*dims):
        return pl.BlockSpec(dims, lambda i, *_: (0,) * len(dims))

    vector = whole(1, width)
    return call(
        attend_body,
        2 * images * keys * width * 2 * inner * 13 // 10,
        images * (media_rows * width * 2 + 2 * keys * width * 2),
        grid_spec=pltpu.PrefetchScalarGridSpec(
            num_scalar_prefetch=2,
            grid=(images,),
            in_specs=[
                image(media_rows, width), whole(rows, width), whole(width, inner),
                whole(width, 2 * inner), vector, vector, vector, vector,
            ],
            out_specs=[
                pl.BlockSpec((media_rows, width), lambda i, *_: (i, 0)), whole(rows, width),
                image(keys, 2 * inner), whole(rows, inner),
                pl.BlockSpec((latent_rows, inner), lambda i, *_: (i, 0)), image(1, inner),
            ],
            scratch_shapes=[pltpu.VMEM((rows, 2 * inner), bf16)],
        ),
        out_shape=[
            shape((images * media_rows, width), bf16),
            shape((rows, width), bf16),
            shape((images, keys, 2 * inner), bf16),
            shape((rows, inner), bf16),
            shape((rows, inner), bf16),
            shape((images, 1, inner), f32),
        ],
    )(lengths, mine, media, latents, query_weight, keyval_weight, *gains)


def split_rows(source, targets, mine, shards):
    size = source.shape[0] // shards
    low = jnp.bitwise_and(mine, shards - 1)
    for k in range(shards // 2):
        for which in range(2):
            at = pl.multiple_of(jnp.bitwise_xor(low, 2 * k + which) * size, size)
            targets[which][pl.ds(k * size, size), :] = source[pl.ds(at, size), :]


def erf_parts(values):
    z = jnp.abs(values) * (0.5 ** 0.5)
    below = 1.0 + 0.3275911 * z
    t = pl.reciprocal(below, approx=True)
    t = t * (2.0 - below * t)
    density = jnp.exp(-z * z)
    tail = t * (0.127414796 + t * (-0.142248368 + t * (0.7107068705 + t * (-0.7265760135 + t * 0.5307027145))))
    tail = tail * density
    return jnp.where(values < 0, tail, 1.0 - tail), density * 0.3989422804014327


def feed_body(
    shards, mine, mixed, latents, output_weight, feed_gain, feed_bias, cotangent, inner_weight,
    outer_weight, residual, turned, slope, outer_grad, result, hidden, flipped, total,
):
    step = pl.program_id(0)
    tile = slope.shape[1]

    @pl.when(step == 0)
    def _():
        residual[...] = latents[...].astype(f32) + dot(mixed[...], output_weight[...])
        normed, _ = normalise(residual[...])
        low = normed * feed_gain[...] + feed_bias[...]
        hidden[...] = low.astype(bf16)
        flipped[...] = jnp.transpose(low).astype(bf16)
        split_rows(flipped, (turned.at[0], turned.at[1]), mine[0], shards)

    inner_rows = dot(hidden[...], inner_weight[...])
    below, density = erf_parts(inner_rows)
    slope[...] = (below + inner_rows * density).astype(bf16)
    activation = (inner_rows * below).astype(bf16)
    weight_grad = dot(activation, cotangent[...], 0, 0).astype(bf16)
    size = outer_grad.shape[3]
    for s in range(tile // size):
        outer_grad[s % 2, s // 2, 0] = weight_grad[s * size : (s + 1) * size]
    part = dot(activation, outer_weight[...])

    @pl.when(step == 0)
    def _():
        total[...] = residual[...] + part

    @pl.when(step > 0)
    def _():
        total[...] += part

    @pl.when(step == pl.num_programs(0) - 1)
    def _():
        result[...] = total[...].astype(bf16)


def feed(mine, shards, mixed, latents, output_weight, feed_gain, feed_bias, cotangent,
         inner_weight, outer_weight, tile=1024):
    rows, width = latents.shape
    inner = mixed.shape[1]
    hidden_units = inner_weight.shape[1]
    steps = hidden_units // tile

    def whole(*dims):
        return pl.BlockSpec(dims, lambda t, _: (0,) * len(dims))

    return call(
        functools.partial(feed_body, shards),
        6 * rows * width * hidden_units,
        6 * width * hidden_units + 2 * rows * hidden_units,
        grid_spec=pltpu.PrefetchScalarGridSpec(
            num_scalar_prefetch=1,
            grid=(steps,),
            in_specs=[
                whole(rows, inner), whole(rows, width), whole(inner, width), whole(1, width),
                whole(1, width), whole(rows, width),
                pl.BlockSpec((width, tile), lambda t, _: (0, t)),
                pl.BlockSpec((tile, width), lambda t, _: (t, 0)),
            ],
            out_specs=[
                whole(rows, width), whole(2, width // 2, rows),
                pl.BlockSpec((rows, tile), lambda t, _: (0, t)),
                pl.BlockSpec(
                    (2, shards // steps // 2, 1, hidden_units // shards, width),
                    lambda t, mine: (0, 0, jnp.bitwise_xor(t, mine[0] // (shards // steps)), 0, 0),
                ),
                whole(rows, width),
            ],
            scratch_shapes=[
                pltpu.VMEM((rows, width), bf16), pltpu.VMEM((width, rows), bf16),
                pltpu.VMEM((rows, width), f32),
            ],
        ),
        out_shape=[
            shape((rows, width), f32), shape((2, width // 2, rows), bf16),
            shape((rows, hidden_units), bf16),
            shape((2, shards // steps // 2, steps, hidden_units // shards, width), bf16),
            shape((rows, width), bf16),
        ],
    )(mine, mixed, latents, output_weight, feed_gain, feed_bias, cotangent, inner_weight, outer_weight)


def feed_back_body(
    slope, outer_weight, inner_weight, turned, residual, feed_gain, cotangent, mixed, output_weight,
    *refs,
):
    residual_grad, mixed_grad, output_grad, sums, weight_keep, weight_send, total = refs[-7:]
    step = pl.program_id(0)
    activation_grad = dot(cotangent[...], outer_weight[...], 1, 1)
    inner_grad = (activation_grad * slope[...].astype(f32)).astype(bf16)
    weight_keep[...] = dot(turned[0], inner_grad).astype(bf16)
    weight_send[...] = dot(turned[1], inner_grad).astype(bf16)
    part = dot(inner_grad, inner_weight[...], 1, 1)

    @pl.when(step == 0)
    def _():
        total[...] = part

    @pl.when(step > 0)
    def _():
        total[...] += part

    @pl.when(step == pl.num_programs(0) - 1)
    def _():
        hidden_grad = total[...]
        normed, factor = normalise(residual[...])
        sums[...] = jnp.concatenate(
            [
                jnp.sum(hidden_grad * normed, axis=0, keepdims=True),
                jnp.sum(hidden_grad, axis=0, keepdims=True),
                jnp.zeros((6, hidden_grad.shape[1]), f32),
            ],
            axis=0,
        )
        grad = cotangent[...].astype(f32) + norm_back(hidden_grad, normed, factor, feed_gain[...])
        residual_grad[...] = grad
        low = grad.astype(bf16)
        mixed_grad[...] = dot(low, output_weight[...], 1, 1).astype(bf16)
        output_grad[...] = dot(mixed[...], low, 0, 0).astype(bf16)


def feed_back(slope, outer_weight, inner_weight, turned, residual, feed_gain, cotangent, mixed,
              output_weight, after=(), tile=1024):
    rows, hidden_units = slope.shape
    width = inner_weight.shape[0]
    inner = mixed.shape[1]

    def whole(*dims):
        return pl.BlockSpec(dims, lambda t: (0,) * len(dims))

    return call(
        feed_back_body,
        6 * rows * width * hidden_units + 4 * rows * width * inner,
        2 * hidden_units * (rows + 3 * width) + 8 * rows * width,
        grid=(hidden_units // tile,),
        in_specs=[
            pl.BlockSpec((rows, tile), lambda t: (0, t)),
            pl.BlockSpec((tile, width), lambda t: (t, 0)),
            pl.BlockSpec((width, tile), lambda t: (0, t)),
            whole(2, width // 2, rows), whole(rows, width), whole(1, width), whole(rows, width),
            whole(rows, inner), whole(inner, width),
        ] + unread(after),
        out_specs=[
            whole(rows, width), whole(rows, inner), whole(inner, width), whole(8, width),
        ] + [pl.BlockSpec((width // 2, tile), lambda t: (0, t))] * 2,
        scratch_shapes=[pltpu.VMEM((rows, width), f32)],
        out_shape=[
            shape((rows, width), f32), shape((rows, inner), bf16), shape((inner, width), bf16),
            shape((8, width), f32),
        ] + [shape((width // 2, hidden_units), bf16)] * 2,
    )(slope, outer_weight, inner_weight, turned, residual, feed_gain, cotangent, mixed,
      output_weight, *after)


def attend_back_body(lengths, mine, keyval, query, mixed_grad, log_total, *refs):
    media_grads, latent_grads, query_grad = refs[-3:]
    step = pl.program_id(0)
    media_rows = media_grads.shape[0]
    inner = query.shape[1]
    own = own_head()

    def put(columns, values):
        values = values.astype(bf16)
        media_grads[:, columns] = values[:media_rows]
        latent_grads[:, columns] = values[media_rows:]

    for g in range(inner // GROUP):
        at = pl.ds(g * GROUP, GROUP)
        value_at = pl.ds(inner + g * GROUP, GROUP)
        stacked = stack_heads(query[:, at], own)
        scores = score_columns(keyval[0, :, at], stacked, lengths[mine[1] + step], media_rows)
        prob_rows = jnp.exp(scores - log_total[0, :, at])
        stacked_grad = stack_heads(mixed_grad[:, at], own)
        prob_grad = dot(keyval[0, :, value_at], stacked_grad, 1, 1)
        put(value_at, dot(prob_rows.astype(bf16), stacked_grad))
        along = jnp.sum(prob_rows * prob_grad, axis=0, keepdims=True)
        score_grad = (prob_rows * (prob_grad - along)).astype(bf16)
        put(at, dot(score_grad, stacked))
        full = dot(score_grad, keyval[0, :, at], 0, 0)
        query_grad[:, at] = unstack_heads(full, own).astype(bf16)


def attend_back(lengths, mine, keyval, query, mixed_grad, log_total, after=()):
    images, keys, pair = keyval.shape
    rows, inner = query.shape
    latent_rows = rows // images
    media_rows = keys - latent_rows

    def image(count, columns):
        return pl.BlockSpec((1, count, columns), lambda i, *_: (i, 0, 0))

    def flat(count, columns):
        return pl.BlockSpec((count, columns), lambda i, *_: (i, 0))

    return call(
        attend_back_body,
        2 * images * keys * inner * GROUP * 5,
        4 * images * keys * pair,
        grid_spec=pltpu.PrefetchScalarGridSpec(
            num_scalar_prefetch=2,
            grid=(images,),
            in_specs=[
                image(keys, pair), flat(latent_rows, inner), flat(latent_rows, inner), image(1, inner),
            ] + unread(after),
            out_specs=[flat(media_rows, pair), flat(latent_rows, pair), flat(latent_rows, inner)],
        ),
        out_shape=[
            shape((images * media_rows, pair), bf16), shape((rows, pair), bf16),
            shape((rows, inner), bf16),
        ],
    )(lengths, mine, keyval, query, mixed_grad, log_total, *after)


def input_weight_body(
    shards, mine, media_low, media_grads, latent_low, latent_grads, query_grad, feed_sums,
    output_grad, query_weight, keyval_weight, media_gain, media_bias, latent_gain, latent_bias,
    *refs,
):
    packed_keep, packed_send, media_total, sum_rows, product = refs[-5:]
    step = pl.program_id(0)
    width, inner = query_weight.shape

    @pl.when(step == 0)
    def _():
        media_total[...] = jnp.zeros_like(media_total)
        sum_rows[...] = jnp.zeros_like(sum_rows)

    media_total[...] += dot(media_low[...], media_grads[...], 0, 0)
    sum_rows[0:1, :] += jnp.sum(media_grads[...].astype(f32), axis=0, keepdims=True)

    @pl.when(step == pl.num_programs(0) - 1)
    def _():
        latent_total = dot(latent_low[...], latent_grads[...], 0, 0)
        query_total = dot(latent_low[...], query_grad[...], 0, 0) * 0.125
        keyval_rows = keyval_weight[...].astype(f32)
        query_rows = query_weight[...].astype(f32)
        latent_sum = jnp.sum(latent_grads[...].astype(f32), axis=0, keepdims=True)
        query_sum = jnp.sum(query_grad[...].astype(f32), axis=0, keepdims=True) * 0.125

        def along(values):
            return jnp.sum(values, axis=1, keepdims=True)

        turned = jnp.transpose(
            jnp.concatenate(
                [
                    media_gain[...], media_bias[...], latent_gain[...], latent_bias[...],
                    feed_sums[0:4], jnp.zeros((120, width), f32),
                ],
                axis=0,
            )
        )
        media_bias_grad = along(keyval_rows * sum_rows[0:1, :])
        media_gain_grad = (
            along(keyval_rows * media_total[...]) - turned[:, 1:2] * media_bias_grad
        ) / turned[:, 0:1]
        latent_bias_grad = along(keyval_rows * latent_sum) + along(query_rows * query_sum)
        latent_gain_grad = (
            along(keyval_rows * latent_total) + along(query_rows * query_total)
            - turned[:, 3:4] * latent_bias_grad
        ) / turned[:, 2:3]
        lane = lax.broadcasted_iota(jnp.int32, (width, 128), 1)
        packed = jnp.where(lane == 0, media_gain_grad, turned)
        packed = jnp.where(lane == 1, media_bias_grad, packed)
        packed = jnp.where(lane == 2, latent_gain_grad, packed)
        packed = jnp.where(lane == 3, latent_bias_grad, packed)
        pair = 2 * inner
        product[:, :pair] = (media_total[...] + latent_total).astype(bf16)
        product[:, pair : pair + 128] = packed.astype(bf16)
        product[:, pair + 128 : pair + 128 + inner] = query_total.astype(bf16)
        product[:, 2 * pair + 128 :] = jnp.zeros((width, 128), bf16)
        size = inner // shards
        wide = width // 2
        for s in range(shards):
            for part in range(2):
                product[(2 * s + part) * size : (2 * s + part + 1) * size, pair + 128 + inner : 2 * pair + 128] = (
                    output_grad[s * size : (s + 1) * size, part * wide : (part + 1) * wide]
                )
        split_rows(product, (packed_keep, packed_send), mine[0], shards)


def input_weight_grad(mine, shards, media_low, media_grads, latent_low, latent_grads, query_grad,
                      feed_sums, output_grad, query_weight, keyval_weight, gains, after=(), steps=4):
    media_rows, width = media_low.shape
    rows, inner = query_grad.shape
    packed = 4 * inner + 256

    def whole(*dims):
        return pl.BlockSpec(dims, lambda i, _: (0,) * len(dims))

    def part(columns):
        return pl.BlockSpec((media_rows // steps, columns), lambda i, _: (i, 0))

    return call(
        functools.partial(input_weight_body, shards),
        2 * (media_rows + rows) * width * 2 * inner + 2 * rows * width * inner,
        2 * media_rows * (width + 2 * inner),
        grid_spec=pltpu.PrefetchScalarGridSpec(
            num_scalar_prefetch=1,
            grid=(steps,),
            in_specs=[
                part(width), part(2 * inner), whole(rows, width), whole(rows, 2 * inner),
                whole(rows, inner), whole(8, width), whole(inner, width), whole(width, inner),
                whole(width, 2 * inner),
            ] + [whole(1, width)] * 4 + unread(after),
            out_specs=[whole(width // 2, packed)] * 2,
            scratch_shapes=[
                pltpu.VMEM((width, 2 * inner), f32), pltpu.VMEM((8, 2 * inner), f32),
                pltpu.VMEM((width, packed), bf16),
            ],
        ),
        out_shape=[shape((width // 2, packed), bf16)] * 2,
    )(mine, media_low, media_grads, latent_low, latent_grads, query_grad, feed_sums, output_grad,
      query_weight, keyval_weight, *gains, *after)


def media_grad_body(media, media_grads, keyval_weight, media_gain, *refs):
    grad_media = refs[-1]
    norm_grad = dot(media_grads[...], keyval_weight[...], 1, 1)
    normed, factor = normalise(media[0].astype(f32))
    grad_media[0] = norm_back(norm_grad, normed, factor, media_gain[...]).astype(bf16)


def media_grad(media, media_grads, keyval_weight, media_gain, first, count, earlier=None, after=()):
    images, media_rows, width = media.shape
    pair = media_grads.shape[1]
    image = pl.BlockSpec((1, media_rows, width), lambda i: (i + first, 0, 0))
    carried = () if earlier is None else (earlier,)
    return call(
        media_grad_body,
        2 * count * media_rows * width * pair,
        6 * count * media_rows * width,
        grid=(count,),
        in_specs=[
            image, pl.BlockSpec((media_rows, pair), lambda i: (i + first, 0)),
            pl.BlockSpec((width, pair), lambda i: (0, 0)), pl.BlockSpec((1, width), lambda i: (0, 0)),
        ] + unread(carried + tuple(after)),
        out_specs=image,
        out_shape=shape(media.shape, bf16),
        input_output_aliases={4: 0} if carried else {},
    )(media, media_grads, keyval_weight, media_gain, *carried, *after)


def latent_grad_body(
    latents, latent_grads, query_grad, residual_grad, query_weight, keyval_weight, latent_gain, *refs
):
    norm_grad = dot(latent_grads[...], keyval_weight[...], 1, 1)
    norm_grad += dot(query_grad[...], query_weight[...], 1, 1) * 0.125
    normed, factor = normalise(latents[...].astype(f32))
    part = norm_back(norm_grad, normed, factor, latent_gain[...])
    refs[-1][...] = (residual_grad[...] + part).astype(bf16)


def latent_grad(latents, latent_grads, query_grad, residual_grad, query_weight, keyval_weight,
                latent_gain, after=()):
    rows, width = latents.shape
    operands = (latents, latent_grads, query_grad, residual_grad, query_weight, keyval_weight, latent_gain)
    return call(
        latent_grad_body,
        2 * rows * width * 3 * query_grad.shape[1],
        16 * rows * width,
        grid=(1,),
        in_specs=[pl.BlockSpec(v.shape, lambda i: (0, 0)) for v in operands] + unread(after),
        out_specs=pl.BlockSpec((rows, width), lambda i: (0, 0)),
        out_shape=shape((rows, width), bf16),
    )(*operands, *after)


def swap(values, bit, devices):
    pairs = [(d, d ^ (1 << bit)) for d in range(devices)]
    return lax.ppermute(values, ("img_hi", "img_lo", "head_hi", "head_lo"), pairs)


def rounded_sum(*values):
    return sum(v.astype(f32) for v in values).astype(bf16)


def split_sum(dims, which, columns, halves, steps=1):
    block = (dims[0] // steps, *[2 if w is None else 1 for w in which], dims[3], dims[4] // halves)
    place = tuple(0 if w is None else w for w in which)
    return pl.BlockSpec(block, lambda i: (i, *place, 0, columns))


def first_body(keep_a, got_a, keep_b, got_b, *refs):
    send_a, send_b = refs[-2:]
    send_a[...] = rounded_sum(keep_a[:, 0], got_a[:, 0])
    send_b[...] = rounded_sum(keep_b[:, :, 0], got_b[:, :, 0])


def second_body(keep_a, core_a, got_a, keep_b, core_b, got_b, *refs):
    send_a, send_b = refs[-2:]
    send_a[...] = rounded_sum(keep_a[:, 0, 0], core_a[:, 0, 0], got_a[:, 0])
    send_b[...] = rounded_sum(keep_b[:, 0, 0], core_b[:, 0, 0], got_b[:, 0])


def third_body(keep, core, got_a, got_b, more_a, more_b, *refs):
    send, held = refs[-2:]
    half = more_a.shape[-1]
    for z in range(keep.shape[0]):
        target = (held, send)[z % 2]
        for p, (got, more) in enumerate(((got_a, more_a), (got_b, more_b))):
            at = slice(p * half, (p + 1) * half)
            target[z // 2, :, at] = rounded_sum(
                keep[z, 0, 0, :, at], core[z, 0, 0, :, at], got[z, 0], more[z]
            )


def later_body(keep, got, *refs):
    send, held = refs[-2:]
    for z in range(keep.shape[0]):
        (held, send)[z % 2][z // 2] = rounded_sum(keep[z], got[z])


def pick_body(keep, *refs):
    send, held = refs[-2:]
    for z in range(keep.shape[0]):
        (held, send)[z % 2][z // 2] = keep[z]


def pass_on(values, after):
    def nothing(*refs):
        pass

    return call(
        nothing, 0, 0, grid=(1,), in_specs=unread((values, *after)), out_specs=unread((values,))[0],
        out_shape=shape(values.shape, values.dtype), input_output_aliases={0: 0},
    )(values, *after)


class Upper:
    def __init__(self, devices, keep):
        self.devices, self.keep, self.bit, self.got = devices, keep, 2, None

    def add(self, body, operands, specs, outs, out_specs, after, steps=1):
        size = sum(o.size for o in outs)

        def sums(*refs):
            return body(*refs[: len(operands)], *refs[-len(outs) :])

        return call(
            sums, size, 8 * size, grid=(steps,), in_specs=specs + unread(after), out_specs=out_specs,
            out_shape=outs,
        )(*operands, *after)

    def later(self, after=()):
        top, rows, columns = self.keep.shape
        whole = pl.BlockSpec((top, rows, columns), lambda i: (0, 0, 0))
        half = pl.BlockSpec((top // 2, rows, columns), lambda i: (0, 0, 0))
        operands = (self.keep,) if self.got is None else (self.keep, self.got)
        send, self.keep = self.add(
            pick_body if self.got is None else later_body, operands, [whole] * len(operands),
            [shape((top // 2, rows, columns), bf16)] * 2, [half] * 2, after,
        )
        self.bit += 1
        self.got = swap(send, self.bit, self.devices)
        return (send,)

    def total(self):
        return self.keep[0].astype(f32) + self.got[0].astype(f32)


class Halving(Upper):
    def __init__(self, devices, halves):
        keep, send = halves
        rows, columns = keep.shape[0] // (devices // 2), keep.shape[1]
        self.dims = (devices // 8, 2, 2, rows, columns)
        super().__init__(devices, keep.reshape(self.dims))
        self.core = swap(send, 0, devices).reshape(self.dims)

    def first(self, after=()):
        top, _, _, rows, columns = self.dims
        steps = 2 if top % 2 == 0 else 1
        a = split_sum(self.dims, (1, None), 0, 2, steps)
        b = split_sum(self.dims, (None, 1), 1, 2, steps)
        out = pl.BlockSpec((top // steps, 2, rows, columns // 2), lambda i: (i, 0, 0, 0))
        sends = self.add(
            first_body, (self.keep, self.core) * 2, [a, a, b, b],
            [shape((top, 2, rows, columns // 2), bf16)] * 2, [out] * 2, after, steps,
        )
        self.gots = [swap(s, bit, self.devices) for s, bit in zip(sends, (2, 1))]
        return tuple(sends)

    def second(self, after=()):
        top, _, _, rows, columns = self.dims
        a, b = split_sum(self.dims, (0, 1), 0, 2), split_sum(self.dims, (1, 0), 1, 2)
        got = pl.BlockSpec((top, 1, rows, columns // 2), lambda i: (0, 1, 0, 0))
        out = pl.BlockSpec((top, rows, columns // 2), lambda i: (0, 0, 0))
        sends = self.add(
            second_body, (self.keep, self.core, self.gots[0], self.keep, self.core, self.gots[1]),
            [a, a, got, b, b, got], [shape((top, rows, columns // 2), bf16)] * 2, [out] * 2, after,
        )
        self.more = [swap(s, bit, self.devices) for s, bit in zip(sends, (1, 2))]
        return tuple(sends)

    def third(self, after=()):
        top, _, _, rows, columns = self.dims
        here = split_sum(self.dims, (0, 0), 0, 1)
        got = pl.BlockSpec((top, 1, rows, columns // 2), lambda i: (0, 0, 0, 0))
        more = pl.BlockSpec((top, rows, columns // 2), lambda i: (0, 0, 0))
        out = pl.BlockSpec((top // 2, rows, columns), lambda i: (0, 0, 0))
        send, self.keep = self.add(
            third_body, (self.keep, self.core, *self.gots, *self.more),
            [here, here, got, got, more, more], [shape((top // 2, rows, columns), bf16)] * 2,
            [out] * 2, after,
        )
        self.bit = 3
        self.got = swap(send, self.bit, self.devices)
        return (send,)


def natural_share(halves, shards, axes):
    rows, columns = halves[0].shape[0] // (shards // 2), halves[0].shape[1]
    parts = [v.reshape(shards // 2, rows, columns).astype(f32) for v in halves]
    return lax.psum_scatter(
        jnp.stack(parts, axis=1).reshape(-1, columns), axes, scatter_dimension=0, tiled=True
    )


def on_device(
    thin, axes, heads, media_tokens, latents, lengths, query_weight, keyval_weight, output_weight,
    inner_weight, outer_weight, media_gain, media_bias, latent_gain, latent_bias, feed_gain,
    feed_bias, cotangent,
):
    images, media_rows, width = media_tokens.shape
    latent_rows = latents.shape[1]
    inner = query_weight.shape[1]
    shards = 32
    everywhere = sum(axes, ())
    devices = lax.axis_size(everywhere)
    mine = jnp.stack([jnp.int32(0) if thin else lax.axis_index(everywhere), lax.axis_index(heads) * images])
    row = lambda v: v.reshape(1, width)
    flat = lambda v: v.reshape(images * latent_rows, v.shape[2])
    deep = lambda v: v.reshape(images, latent_rows, v.shape[1])

    norms = (row(media_gain), row(media_bias), row(latent_gain), row(latent_bias))
    flat_latents, flat_cotangent = flat(latents), flat(cotangent)
    media_low, latent_low, keyval, query, mixed, log_total = attend(
        lengths, mine, media_tokens, flat_latents, query_weight, keyval_weight, norms
    )
    residual, turned, slope, outer_halves, out_latents = feed(
        mine, shards, mixed, flat_latents, output_weight, row(feed_gain), row(feed_bias),
        flat_cotangent, inner_weight, outer_weight,
    )
    residual_grad, mixed_grad, output_grad, feed_sums, *inner_halves = feed_back(
        slope, outer_weight, inner_weight, turned, residual, row(feed_gain), flat_cotangent, mixed,
        output_weight,
    )
    outer = within = narrow = None
    run = (lambda *_: ()) if thin else (lambda chain, step, after: getattr(chain, step)(after))
    rows_on = lambda values, axis: lax.psum_scatter(values, axis, scatter_dimension=0, tiled=True)
    after = ()
    if not thin:
        within = Halving(devices, inner_halves)
        outer_sum = rows_on(outer_halves.reshape(-1, width), axes[3])
        outer_sum = pass_on(outer_sum, (mixed_grad,))
        after = (outer_sum,)
        outer_sum = rows_on(outer_sum, axes[1] + axes[2])
        outer = Upper(devices, outer_sum.reshape(devices // 8, -1, width))
    media_grads, latent_grads, query_grad = attend_back(
        lengths, mine, keyval, query, mixed_grad, log_total, after
    )
    after = run(within, "first", (query_grad,))
    packed = input_weight_grad(
        mine, shards, media_low, media_grads, latent_low, latent_grads, query_grad, feed_sums,
        output_grad, query_weight, keyval_weight, norms, after,
    )
    after = run(within, "second", tuple(packed))
    if not thin:
        narrow = Halving(devices, (packed[0], pass_on(packed[1], after)))
    after = run(outer, "later", after)
    half = images // 2
    grad_media = media_grad(media_tokens, media_grads, keyval_weight, row(media_gain), 0, half, None, after)
    after = run(narrow, "first", (grad_media,))
    after = run(within, "third", after)
    after = run(outer, "later", after)
    grad_media = media_grad(
        media_tokens, media_grads, keyval_weight, row(media_gain), half, images - half, grad_media,
        after,
    )
    after = run(narrow, "second", (grad_media,))
    after = run(within, "later", after)
    grad_latents = latent_grad(
        flat_latents, latent_grads, query_grad, residual_grad, query_weight, keyval_weight,
        row(latent_gain), after,
    )
    after = run(narrow, "third", (grad_latents,))
    run(narrow, "later", after)
    pair = 2 * inner
    if thin:
        outer_halves = jnp.swapaxes(outer_halves, 1, 2).reshape(2, -1, width)
        grad_outer = natural_share((outer_halves[0], outer_halves[1]), shards, everywhere)
        grad_inner = natural_share(inner_halves, shards, everywhere)
        rest = natural_share([v[:, : pair + 128 + inner] for v in packed], shards, everywhere)
        grad_output = lax.psum_scatter(output_grad.astype(f32), everywhere, scatter_dimension=0, tiled=True)
    else:
        grad_outer, grad_inner, rest = outer.total(), within.total(), narrow.total()
        grad_output = rest[:, pair + 128 + inner : 2 * pair + 128]
        size = inner // devices
        grad_output = jnp.concatenate([grad_output[:size], grad_output[size:]], axis=1)
    grad_keyval, sums, grad_query = rest[:, :pair], rest[:, pair : pair + 128], rest[:, pair + 128 : pair + 128 + inner]
    return (
        deep(out_latents), grad_media, deep(grad_latents), grad_query, grad_keyval, grad_output,
        grad_inner, grad_outer, sums[:, 0], sums[:, 1], sums[:, 2], sums[:, 3], sums[:, 4], sums[:, 5],
    )


def solution(mesh):
    images, heads = mesh.shape["img"], mesh.shape["head"]
    thin = mesh.size != 32 or images % 2 != 0 or heads % 2 != 0
    if thin:
        axes, own = (("img",), (), ("head",), ()), "head"
    else:
        sizes = (images // 2, 2, heads // 2, 2)
        mesh = jax.sharding.Mesh(mesh.devices.reshape(sizes), ("img_hi", "img_lo", "head_hi", "head_lo"))
        axes, own = (("img_hi",), ("img_lo",), ("head_hi",), ("head_lo",)), ("head_hi", "head_lo")
    everywhere, first = sum(axes, ()), axes[0] + axes[1]
    spread = P(everywhere, None, None)
    return jax.shard_map(
        functools.partial(on_device, thin, axes, own),
        mesh=mesh,
        in_specs=(spread, spread, P(first)) + (P(),) * 11 + (spread,),
        out_specs=(spread,) * 3 + (P(everywhere, None),) * 5 + (P(everywhere),) * 6,
        check_vma=False,
    )
```

time: 395 us -> 260 us (0.66)
  waiting for transfers between devices: 121 us -> 25 us
  starting transfers between devices: 54.9 us -> 19.1 us
  between operations: 1.29 us -> 14.2 us
  local copies, waits for them, and re-layouts: 25.3 us -> 12.8 us
  other arithmetic: 13.2 us -> 3.88 us
  Pallas kernels: 177 us -> 184 us
    ppermute x40 -> x16, waiting for transfers between devices: 121 us -> 25 us  [swap(): lax.ppermute(values, ('img_hi', 'img_lo', 'head_hi', 'head_lo'), pairs)]
    ppermute x40 -> x16, starting transfers between devices: 54.9 us -> 18.8 us  [swap(): lax.ppermute(values, ('img_hi', 'img_lo', 'head_hi', 'head_lo'), pairs)]
    slice x16 -> x4, local copies, waits for them, and re-layouts: 12.1 us -> 2.08 us  [the longest x1 0.78 us: on_device(): sums[:, 5]]
    convert_element_type x35 -> x0, other arithmetic: 5.89 us -> none  [add(): return (left.astype(f32) + right.astype(f32)).astype(dtype)]
    pallas_call x9 -> x19, Pallas kernels: 147 us -> 153 us  [the longest x1 29.8 us: feed(): call(functools.partial(feed_body, shards), 6 * rows * width * hidden_unit...]
    unnamed x38 -> x34, local copies, waits for them, and re-layouts: 10.4 us -> 10.7 us
  transfers between devices with their start and end apart: 40 -> 18, of which waited for: 27 -> 4; matrix products, arithmetic and copies ran while one was open for 7% -> 1% of each run, Pallas kernels for 19% -> 47%
where the time goes in v2:
time: 260 us; the launch traced here: 259 us
  Pallas kernels  184 us (71%)
  waiting for transfers between devices  25 us (10%)
  starting transfers between devices  19.1 us (7%)
  between operations  14.2 us (5%)
  local copies, waits for them, and re-layouts  12.8 us (5%)
  other arithmetic  3.88 us (1%)
    pallas_call x1, Pallas kernels, attend(): call(attend_body, 2 * images * keys * width * 2 * inner * 13 // 10, image...  31.3 us
    pallas_call x1, Pallas kernels, feed(): call(functools.partial(feed_body, shards), 6 * rows * width * hidden_unit...  29.8 us
    pallas_call x10, Pallas kernels, add(): call(sums, size, 8 * size, grid=(steps,), in_specs=specs + unread(after),...  25.5 us
    pallas_call x1, Pallas kernels, input_weight_grad(): call(functools.partial(input_weight_body, shards), 2 * (media_rows + rows...  25.3 us
    pallas_call x1, Pallas kernels, feed_back(): call(feed_back_body, 6 * rows * width * hidden_units + 4 * rows * width *...  25.3 us
    ppermute x16, waiting for transfers between devices, swap(): lax.ppermute(values, ('img_hi', 'img_lo', 'head_hi', 'head_lo'), pairs)  25 us
    pallas_call x2, Pallas kernels, media_grad(): call(media_grad_body, 2 * count * media_rows * width * pair, 6 * count *...  24 us
    ppermute x16, starting transfers between devices, swap(): lax.ppermute(values, ('img_hi', 'img_lo', 'head_hi', 'head_lo'), pairs)  18.8 us
  transfers between devices with their start and end apart: 18, of which 4 were waited for; matrix products, arithmetic and copies ran while one was open for 1% of the time, Pallas kernels for 47%

profile of v2, /device:TPU:0, one launch (start us, length us, event | category | flops | bytes accessed | tf_op | source)
XLA Modules:
  0.0 259.1 jit_solution(14419105759253539584)
XLA Ops:
  7.8 31.3 %shard_map.254 = (bf16[4608,1024]{1,0:T(8,128)(2,1)}, bf16[512,1024]{1,0:T(8,128)(2,1)}, bf16[8,640,1024]{2,1,0:T(8,128)(2,1)}, bf16[512,512]{1,0:T(8,128)(2,1)}...) custom-call(s32[32]{0:T(128)} %lengths.3, s32[2]{0:T(128)} %pad_add_fusion.mine, bf16[8,576,1024]{2,1,0:T(8,128)(2,1)} %media.5, ...), custom_call_target="tpu_custom_call" | custom-call | flops 13958643712 | bytes 30408704 | tf_op jit(solution)/shard_map/pallas_call | solution.py:130
  39.1 29.8 %shard_map.255 = (f32[512,1024]{1,0:T(8,128)}, bf16[2,512,512]{2,1,0:T(8,128)(2,1)}, bf16[512,4096]{1,0:T(8,128)(2,1)}, bf16[2,4,4,128,1024]{4,3,2,1,0:T(8,128)(2,1)}, bf16[512,1024]{1,0:T(8,128)(2,1)}) custom-call(s32[2]{0:T(128)} %pad_add_fusion.mine, bf16[512,512]{1,0:T(8,128)(2,1)} %get-tuple-element.56.mixed, bf16[512,1024]{1,0:T(8,128)(2,1)} %bitcast.48, ...), custom_call_target="tpu_custom_call" | custom-call | flops 12884901888 | bytes 29360128 | tf_op jit(solution)/shard_map/pallas_call | solution.py:228
  69.2 25.3 %shard_map.256 = (f32[512,1024]{1,0:T(8,128)}, bf16[512,512]{1,0:T(8,128)(2,1)}, bf16[512,1024]{1,0:T(8,128)(2,1)}, f32[8,1024]{1,0:T(8,128)}, bf16[512,4096]{1,0:T(8,128)(2,1)}, /*index=5*/bf16[512,4096]{1,0:T(8,128)(2,1)}) custom-call(bf16[512,4096]{1,0:T(8,128)(2,1)} %get-tuple-element.60.slope, bf16[4096,1024]{1,0:T(8,128)(2,1)} %outer_weight.3, ...), custom_call_target="tpu_custom_call" | custom-call | flops 13958643712 | bytes 33554432 | tf_op jit(solution)/shard_map/pallas_call | solution.py:312
  95.1 16.0 %shard_map.258 = (bf16[4608,1024]{1,0:T(8,128)(2,1)}, bf16[512,1024]{1,0:T(8,128)(2,1)}, bf16[512,512]{1,0:T(8,128)(2,1)}) custom-call(s32[32]{0:T(128)} %lengths.3, s32[2]{0:T(128)} %pad_add_fusion.mine, bf16[8,640,1024]{2,1,0:T(8,128)(2,1)} %get-tuple-element.58.keyval, bf16[512,512]{1,0:T(8,128)(2,1)} %get-tuple-element.59.query, ...), custom_call_target="tpu_custom_call" | custom-call | flops 6710886400 | bytes 20971520 | tf_op jit(solution)/shard_map/pallas_call | solution.py:376
  111.2 2.0 copy-done
  113.1 3.4 %shard_map.259 = (bf16[4,2,32,2048]{3,2,1,0:T(8,128)(2,1)}, bf16[4,2,32,2048]{3,2,1,0:T(8,128)(2,1)}) custom-call(bf16[4,2,2,32,4096]{4,3,2,1,0:T(8,128)(2,1)} %bitcast.24, bf16[4,2,2,32,4096]{4,3,2,1,0:T(8,128)(2,1)} %bitcast.29, bf16[4,2,2,32,4096]{4,3,2,1,0:T(8,128)(2,1)} %bitcast.25, bf16[4,2,2,32,4096]{4,3,2,1,0:T(8,128)(2,1)} %bitcast.30, ...), custom_call_target="tpu_custom_call" | custom-call | flops 1048576 | bytes 8388608 | tf_op jit(solution)/shard_map/pallas_call | solution.py:620
  116.5 2.8 %collective-permute-start.1 = (bf16[4,2,32,2048]{3,2,1,0:T(8,128)(2,1)}, bf16[4,2,32,2048]{3,2,1,0:T(8,128)(2,1)S(1)}, u32[]{:S(2)}, u32[]{:S(2)}) collective-permute-start(bf16[4,2,32,2048]{3,2,1,0:T(8,128)(2,1)} %get-tuple-element.70.refs_0_), channel_id=1, source_target_pairs={{0,4},{1,5},{2,6},{3,7},{4,0},{5,1},{6,2},{7,3},{8,12},{9,13},{10,... | collective-permute-start | bytes 3145736 | tf_op jit(solution)/shard_map/ppermute | solution.py:551
  119.3 1.7 collective-permute-start.2
  121.0 25.3 %shard_map.260 = (bf16[512,2304]{1,0:T(8,128)(2,1)}, bf16[512,2304]{1,0:T(8,128)(2,1)}) custom-call(s32[2]{0:T(128)} %pad_add_fusion.mine, bf16[4608,1024]{1,0:T(8,128)(2,1)} %get-tuple-element.72.media_low, bf16[4608,1024]{1,0:T(8,128)(2,1)} %get-tuple-element.66.media_grads, bf16[512,1024]{1,0:T(8,128)(2,1)} %get-tuple-element.73.latent_low, ...), custom_call_target="tpu_custom_call" | custom-call | flops 11274289152 | bytes 18874368 | tf_op jit(solution)/shard_map/pallas_call | solution.py:474
  146.3 11.2 %collective-permute-done.1.refs_2_ = bf16[4,2,32,2048]{3,2,1,0:T(8,128)(2,1)S(1)} collective-permute-done((bf16[4,2,32,2048]{3,2,1,0:T(8,128)(2,1)}, bf16[4,2,32,2048]{3,2,1,0:T(8,128)(2,1)S(1)}, u32[]{:S(2)}, u32[]{:S(2)}) %collective-permute-start.1) | collective-permute-done | bytes 1048608 | tf_op jit(solution)/shard_map/ppermute | solution.py:551
  158.8 3.0 %shard_map.261 = (bf16[4,32,2048]{2,1,0:T(8,128)(2,1)}, bf16[4,32,2048]{2,1,0:T(8,128)(2,1)}) custom-call(bf16[4,2,2,32,4096]{4,3,2,1,0:T(8,128)(2,1)} %bitcast.26, bf16[4,2,2,32,4096]{4,3,2,1,0:T(8,128)(2,1)} %bitcast.31, bf16[4,2,32,2048]{3,2,1,0:T(8,128)(2,1)} %copy-done.2, bf16[4,2,2,32,4096]{4,3,2,1,0:T(8,128)(2,1)} %bitcast.27, ...), custom_call_target="tpu_custom_call" | custom-call | flops 524288 | bytes 4194304 | tf_op jit(solution)/shard_map/pallas_call | solution.py:620
  162.8 1.6 collective-permute-start.4
  165.1 2.2 shard_map.262
  167.3 1.5 collective-permute-start.3
  168.8 12.0 %shard_map.263.refs_4_.refs_0_ = bf16[8,576,1024]{2,1,0:T(8,128)(2,1)} custom-call(bf16[8,576,1024]{2,1,0:T(8,128)(2,1)} %media.5, bf16[4608,1024]{1,0:T(8,128)(2,1)} %get-tuple-element.66.media_grads, bf16[1024,1024]{1,0:T(8,128)(2,1)} %keyval_weight.9, f32[1,1024]{1,0:T(1,128)} %bitcast.52, bf16[2,128,1024]{2,1,0:T(8,128)(2,1)} %get-tuple-element.81.refs_0_), custom_call_target="tpu_custom_call" | custom-call | flops 4831838208 | bytes 14155776 | tf_op jit(solution)/shard_map/pallas_call | solution.py:509
  180.8 1.4 copy-done.1
  182.2 2.5 shard_map.265
  184.7 1.4 collective-permute-start.8
  186.6 3.5 %shard_map.266 = (bf16[2,32,4096]{2,1,0:T(8,128)(2,1)}, bf16[2,32,4096]{2,1,0:T(8,128)(2,1)}) custom-call(bf16[4,2,2,32,4096]{4,3,2,1,0:T(8,128)(2,1)} %bitcast.28, bf16[4,2,2,32,4096]{4,3,2,1,0:T(8,128)(2,1)} %bitcast.33, bf16[4,2,32,2048]{3,2,1,0:T(8,128)(2,1)} %copy-done.2, bf16[4,2,32,2048]{3,2,1,0:T(8,128)(2,1)} %copy-done.3, ...), custom_call_target="tpu_custom_call" | custom-call | flops 524288 | bytes 4194304 | tf_op jit(solution)/shard_map/pallas_call | solution.py:620
  191.4 2.1 shard_map.267
  193.4 12.0 %shard_map.268.refs_6_ = bf16[8,576,1024]{2,1,0:T(8,128)(2,1)} custom-call(bf16[8,576,1024]{2,1,0:T(8,128)(2,1)} %media.5, bf16[4608,1024]{1,0:T(8,128)(2,1)} %get-tuple-element.66.media_grads, bf16[1024,1024]{1,0:T(8,128)(2,1)} %keyval_weight.9, f32[1,1024]{1,0:T(1,128)} %bitcast.53, ...), custom_call_target="tpu_custom_call", output_to_operand_aliasing={{}: (4, {})} | custom-call | flops 4831838208 | bytes 14155776 | tf_op jit(solution)/shard_map/pallas_call | solution.py:509
  207.1 2.3 shard_map.269
  209.4 1.6 collective-permute-start.10
  211.7 2.4 collective-permute-start.15
  214.9 2.1 shard_map.270
  217.0 6.9 %shard_map.271.refs_6_ = bf16[512,1024]{1,0:T(8,128)(2,1)} custom-call(bf16[512,1024]{1,0:T(8,128)(2,1)} %bitcast.49, bf16[512,1024]{1,0:T(8,128)(2,1)} %get-tuple-element.74.latent_grads, bf16[512,512]{1,0:T(8,128)(2,1)} %get-tuple-element.69.refs_4_.query_grad, f32[512,1024]{1,0:T(8,128)} %get-tuple-element.87.residual_grad, ...), custom_call_target="tpu_custom_call" | custom-call | flops 1610612736 | bytes 8388608 | tf_op jit(solution)/shard_map/pallas_call | solution.py:538
  225.3 2.6 %shard_map.272 = (bf16[2,32,2304]{2,1,0:T(8,128)(2,1)}, bf16[2,32,2304]{2,1,0:T(8,128)(2,1)}) custom-call(bf16[4,2,2,32,2304]{4,3,2,1,0:T(8,128)(2,1)} %bitcast.38, bf16[4,2,2,32,2304]{4,3,2,1,0:T(8,128)(2,1)} %bitcast.43, bf16[4,2,32,1152]{3,2,1,0:T(8,128)(2,1)} %copy-done.4, bf16[4,2,32,1152]{3,2,1,0:T(8,128)(2,1)} %copy-done.5, ...), custom_call_target="tpu_custom_call" | custom-call | flops 294912 | bytes 2359296 | tf_op jit(solution)/shard_map/pallas_call | solution.py:620
  227.9 1.5 collective-permute-start.12
  230.8 7.7 %collective-permute-done.12.refs_1_ = bf16[2,32,2304]{2,1,0:T(8,128)(2,1)S(1)} collective-permute-done((bf16[2,32,2304]{2,1,0:T(8,128)(2,1)}, bf16[2,32,2304]{2,1,0:T(8,128)(2,1)S(1)}, u32[]{:S(2)}, u32[]{:S(2)}) %collective-permute-start.12) | collective-permute-done | bytes 294944 | tf_op jit(solution)/shard_map/ppermute | solution.py:551
  239.2 1.8 shard_map.273
  242.7 5.9 %collective-permute-done.13 = bf16[1,32,2304]{2,1,0:T(8,128)(2,1)S(1)} collective-permute-done((bf16[1,32,2304]{2,1,0:T(8,128)(2,1)}, bf16[1,32,2304]{2,1,0:T(8,128)(2,1)S(1)}, u32[]{:S(2)}, u32[]{:S(2)}) %collective-permute-start.13) | collective-permute-done | bytes 147488 | tf_op jit(solution)/shard_map/ppermute | solution.py:551
  248.5 1.0 add_bitcast_fusion.2
  (69 shorter events, 17.4 us)
Async XLA Ops:
  7.2 87.3 %reduce-scatter.3.cloned.1.call-start = ((), (), s32[]{:S(2)}) async-start(), calls=%async_computation.2 | async-start | bytes 12582912 | tf_op jit(solution)/shard_map/reduce_scatter | solution.py:730
  68.9 96.1 %reduce-scatter.5.cloned.1.call-start = ((), (), s32[]{:S(2)}) async-start(), calls=%async_computation.3 | async-start | bytes 5242880 | tf_op jit(solution)/shard_map/reduce_scatter | solution.py:730
  94.5 16.7 %collective-permute-start = (bf16[512,4096]{1,0:T(8,128)(2,1)}, bf16[512,4096]{1,0:T(8,128)(2,1)S(1)}, u32[]{:S(2)}, u32[]{:S(2)}) collective-permute-start(bf16[512,4096]{1,0:T(8,128)(2,1)} %get-tuple-element.68), channel_id=1, source_target_pairs={{0,1},{1,0},{2,3},{3,2},{4,5},{5,4},{6,7},{7,6},{8,9},{9,8},{10,11... | collective-permute-start | bytes 12582920 | tf_op jit(solution)/shard_map/ppermute | solution.py:551
  111.2 2.0 copy-start
  116.5 40.9 %collective-permute-start.1 = (bf16[4,2,32,2048]{3,2,1,0:T(8,128)(2,1)}, bf16[4,2,32,2048]{3,2,1,0:T(8,128)(2,1)S(1)}, u32[]{:S(2)}, u32[]{:S(2)}) collective-permute-start(bf16[4,2,32,2048]{3,2,1,0:T(8,128)(2,1)} %get-tuple-element.70.refs_0_), channel_id=1, source_target_pairs={{0,4},{1,5},{2,6},{3,7},{4,0},{5,1},{6,2},{7,3},{8,12},{9,13},{10,... | collective-permute-start | bytes 3145736 | tf_op jit(solution)/shard_map/ppermute | solution.py:551
  119.3 38.4 %collective-permute-start.2 = (bf16[4,2,32,2048]{3,2,1,0:T(8,128)(2,1)}, bf16[4,2,32,2048]{3,2,1,0:T(8,128)(2,1)S(1)}, u32[]{:S(2)}, u32[]{:S(2)}) collective-permute-start(bf16[4,2,32,2048]{3,2,1,0:T(8,128)(2,1)} %get-tuple-element.71.refs_1_), channel_id=1, source_target_pairs={{0,2},{1,3},{2,0},{3,1},{4,6},{5,7},{6,4},{7,5},{8,10},{9,11},{10,... | collective-permute-start | bytes 3145736 | tf_op jit(solution)/shard_map/ppermute | solution.py:551
  157.4 1.0 copy-start.2
  157.7 1.1 copy-start.3
  161.8 1.0 copy-start.7
  161.8 2.6 %copy-start.6 = (bf16[4,32,2048]{2,1,0:T(8,128)(2,1)S(1)}, bf16[4,32,2048]{2,1,0:T(8,128)(2,1)}, u32[]{:S(2)}) copy-start(bf16[4,32,2048]{2,1,0:T(8,128)(2,1)} %get-tuple-element.80.refs_2_) | copy-start | bytes 1572868
  161.8 19.0 %collective-permute-start.6 = (bf16[512,2304]{1,0:T(8,128)(2,1)}, bf16[512,2304]{1,0:T(8,128)(2,1)S(1)}, u32[]{:S(2)}, u32[]{:S(2)}) collective-permute-start(bf16[512,2304]{1,0:T(8,128)(2,1)} %shard_map.264), channel_id=1, source_target_pairs={{0,1},{1,0},{2,3},{3,2},{4,5},{5,4},{6,7},{7,6},{8,9},{9,8},{10,11... | collective-permute-start | bytes 7077896 | tf_op jit(solution)/shard_map/ppermute | solution.py:551
  162.8 23.8 %collective-permute-start.4 = (bf16[4,32,2048]{2,1,0:T(8,128)(2,1)S(1)}, bf16[4,32,2048]{2,1,0:T(8,128)(2,1)}, u32[]{:S(2)}, u32[]{:S(2)}) collective-permute-start(bf16[4,32,2048]{2,1,0:T(8,128)(2,1)S(1)} %copy-done.7), channel_id=1, source_target_pairs={{0,2},{1,3},{2,0},{3,1},{4,6},{5,7},{6,4},{7,5},{8,10},{9,11},{10,... | collective-permute-start | bytes 1572872 | tf_op jit(solution)/shard_map/ppermute | solution.py:551
  164.4 22.2 %collective-permute-start.5 = (bf16[4,32,2048]{2,1,0:T(8,128)(2,1)S(1)}, bf16[4,32,2048]{2,1,0:T(8,128)(2,1)}, u32[]{:S(2)}, u32[]{:S(2)}) collective-permute-start(bf16[4,32,2048]{2,1,0:T(8,128)(2,1)S(1)} %copy-done.6), channel_id=1, source_target_pairs={{0,4},{1,5},{2,6},{3,7},{4,0},{5,1},{6,2},{7,3},{8,12},{9,13},{10,... | collective-permute-start | bytes 1572872 | tf_op jit(solution)/shard_map/ppermute | solution.py:551
  167.3 23.3 %collective-permute-start.3 = (bf16[2,128,1024]{2,1,0:T(8,128)(2,1)}, bf16[2,128,1024]{2,1,0:T(8,128)(2,1)S(1)}, u32[]{:S(2)}, u32[]{:S(2)}) collective-permute-start(bf16[2,128,1024]{2,1,0:T(8,128)(2,1)} %get-tuple-element.81.refs_0_), channel_id=1, source_target_pairs={{0,8},{1,9},{2,10},{3,11},{4,12},{5,13},{6,14},{7,15},{8,0},{9,1},... | collective-permute-start | bytes 1572872 | tf_op jit(solution)/shard_map/ppermute | solution.py:551
  180.7 1.4 copy-start.1
  184.7 20.8 %collective-permute-start.8 = (bf16[4,2,32,1152]{3,2,1,0:T(8,128)(2,1)}, bf16[4,2,32,1152]{3,2,1,0:T(8,128)(2,1)S(1)}, u32[]{:S(2)}, u32[]{:S(2)}) collective-permute-start(bf16[4,2,32,1152]{3,2,1,0:T(8,128)(2,1)} %get-tuple-element.83.refs_6_), channel_id=1, source_target_pairs={{0,4},{1,5},{2,6},{3,7},{4,0},{5,1},{6,2},{7,3},{8,12},{9,13},{10,... | collective-permute-start | bytes 1769480 | tf_op jit(solution)/shard_map/ppermute | solution.py:551
  186.1 19.4 %collective-permute-start.9 = (bf16[4,2,32,1152]{3,2,1,0:T(8,128)(2,1)}, bf16[4,2,32,1152]{3,2,1,0:T(8,128)(2,1)S(1)}, u32[]{:S(2)}, u32[]{:S(2)}) collective-permute-start(bf16[4,2,32,1152]{3,2,1,0:T(8,128)(2,1)} %get-tuple-element.84.refs_7_), channel_id=1, source_target_pairs={{0,2},{1,3},{2,0},{3,1},{4,6},{5,7},{6,4},{7,5},{8,10},{9,11},{10,... | collective-permute-start | bytes 1769480 | tf_op jit(solution)/shard_map/ppermute | solution.py:551
  190.1 24.0 %collective-permute-start.7 = (bf16[2,32,4096]{2,1,0:T(8,128)(2,1)}, bf16[2,32,4096]{2,1,0:T(8,128)(2,1)S(1)}, u32[]{:S(2)}, u32[]{:S(2)}) collective-permute-start(bf16[2,32,4096]{2,1,0:T(8,128)(2,1)} %get-tuple-element.85.refs_2_), channel_id=1, source_target_pairs={{0,8},{1,9},{2,10},{3,11},{4,12},{5,13},{6,14},{7,15},{8,0},{9,1},... | collective-permute-start | bytes 1572872 | tf_op jit(solution)/shard_map/ppermute | solution.py:551
  190.6 0.8 copy-start.8
  205.4 6.2 %copy-start.16 = (bf16[1,128,1024]{2,1,0:T(8,128)(2,1)S(1)}, bf16[1,128,1024]{2,1,0:T(8,128)(2,1)}, u32[]{:S(2)}) copy-start(bf16[1,128,1024]{2,1,0:T(8,128)(2,1)} %get-tuple-element.86.refs_1_) | copy-start | bytes 786436
  205.4 0.8 copy-start.4
  206.3 0.8 copy-start.5
  209.4 14.4 %collective-permute-start.10 = (bf16[4,32,1152]{2,1,0:T(8,128)(2,1)}, bf16[4,32,1152]{2,1,0:T(8,128)(2,1)S(1)}, u32[]{:S(2)}, u32[]{:S(2)}) collective-permute-start(bf16[4,32,1152]{2,1,0:T(8,128)(2,1)} %get-tuple-element.89.refs_2_), channel_id=1, source_target_pairs={{0,2},{1,3},{2,0},{3,1},{4,6},{5,7},{6,4},{7,5},{8,10},{9,11},{10,... | collective-permute-start | bytes 884744 | tf_op jit(solution)/shard_map/ppermute | solution.py:551
  211.0 12.8 %collective-permute-start.11 = (bf16[4,32,1152]{2,1,0:T(8,128)(2,1)}, bf16[4,32,1152]{2,1,0:T(8,128)(2,1)S(1)}, u32[]{:S(2)}, u32[]{:S(2)}) collective-permute-start(bf16[4,32,1152]{2,1,0:T(8,128)(2,1)} %get-tuple-element.90.refs_3_), channel_id=1, source_target_pairs={{0,4},{1,5},{2,6},{3,7},{4,0},{5,1},{6,2},{7,3},{8,12},{9,13},{10,... | collective-permute-start | bytes 884744 | tf_op jit(solution)/shard_map/ppermute | solution.py:551
  211.7 18.2 %collective-permute-start.15 = (bf16[1,128,1024]{2,1,0:T(8,128)(2,1)S(1)}, bf16[1,128,1024]{2,1,0:T(8,128)(2,1)S(1)}, u32[]{:S(2)}, u32[]{:S(2)}) collective-permute-start(bf16[1,128,1024]{2,1,0:T(8,128)(2,1)S(1)} %copy-done.16), channel_id=1, source_target_pairs={{0,16},{1,17},{2,18},{3,19},{4,20},{5,21},{6,22},{7,23},{8,24},{9,... | collective-permute-start | bytes 786440 | tf_op jit(solution)/shard_map/ppermute | solution.py:551
  214.1 0.8 copy-start.9
  223.8 5.6 %copy-start.13 = (bf16[1,32,4096]{2,1,0:T(8,128)(2,1)S(1)}, bf16[1,32,4096]{2,1,0:T(8,128)(2,1)}, u32[]{:S(2)}) copy-start(bf16[1,32,4096]{2,1,0:T(8,128)(2,1)} %get-tuple-element.91.refs_0_) | copy-start | bytes 786436
  223.8 6.1 %copy-start.14 = (bf16[1,128,1024]{2,1,0:T(8,128)(2,1)S(1)}, bf16[1,128,1024]{2,1,0:T(8,128)(2,1)}, u32[]{:S(2)}) copy-start(bf16[1,128,1024]{2,1,0:T(8,128)(2,1)} %get-tuple-element.97) | copy-start | bytes 786436
  223.8 18.0 %copy-start.15 = (bf16[1,32,4096]{2,1,0:T(8,128)(2,1)S(1)}, bf16[1,32,4096]{2,1,0:T(8,128)(2,1)}, u32[]{:S(2)}) copy-start(bf16[1,32,4096]{2,1,0:T(8,128)(2,1)} %get-tuple-element.96) | copy-start | bytes 786436
  227.9 10.6 %collective-permute-start.12 = (bf16[2,32,2304]{2,1,0:T(8,128)(2,1)}, bf16[2,32,2304]{2,1,0:T(8,128)(2,1)S(1)}, u32[]{:S(2)}, u32[]{:S(2)}) collective-permute-start(bf16[2,32,2304]{2,1,0:T(8,128)(2,1)} %get-tuple-element.93.refs_2_), channel_id=1, source_target_pairs={{0,8},{1,9},{2,10},{3,11},{4,12},{5,13},{6,14},{7,15},{8,0},{9,1},... | collective-permute-start | bytes 884744 | tf_op jit(solution)/shard_map/ppermute | solution.py:551
  229.4 12.4 %collective-permute-start.14 = (bf16[1,32,4096]{2,1,0:T(8,128)(2,1)S(1)}, bf16[1,32,4096]{2,1,0:T(8,128)(2,1)S(1)}, u32[]{:S(2)}, u32[]{:S(2)}) collective-permute-start(bf16[1,32,4096]{2,1,0:T(8,128)(2,1)S(1)} %copy-done.13), channel_id=1, source_target_pairs={{0,16},{1,17},{2,18},{3,19},{4,20},{5,21},{6,22},{7,23},{8,24},{9,... | collective-permute-start | bytes 786440 | tf_op jit(solution)/shard_map/ppermute | solution.py:551
  241.0 7.5 %collective-permute-start.13 = (bf16[1,32,2304]{2,1,0:T(8,128)(2,1)}, bf16[1,32,2304]{2,1,0:T(8,128)(2,1)S(1)}, u32[]{:S(2)}, u32[]{:S(2)}) collective-permute-start(bf16[1,32,2304]{2,1,0:T(8,128)(2,1)} %get-tuple-element.95), channel_id=1, source_target_pairs={{0,16},{1,17},{2,18},{3,19},{4,20},{5,21},{6,22},{7,23},{8,24},{9,... | collective-permute-start | bytes 442376 | tf_op jit(solution)/shard_map/ppermute | solution.py:551
  (3 other events, 2.1 us)
Sparse Core Ops, SparseCore 0:
  69.0 19.4 reduce-scatter.2
  94.6 69.0 reduce-scatter.4
